TPU v7x, 128 devices: a whole 4x4x4 slice. The times are simulated.
128 devices in a mesh: area: 4 (over y), dev: 32 (over z, x, core).
Axes of the slice: x: 4, y: 4, z: 4, core: 2. Of those that a mesh axis runs over, the one named last changes fastest.
Arguments:
- initial_state: float32 [3, 2097152], P(None, ('area', 'dev')), may hold values from -7 to 0.9, as said below
- waveform_guess: bfloat16 [10, 2097152], P(None, ('area', 'dev')), may hold values from -7 to -2
- drive_current: float32 [10, 2097152], P(None, ('area', 'dev')), may hold values from -6 to 6
- conductance: bfloat16 [8, 128, 128], replicated, may hold values from 0 to 0.31, as said below
- partners: int32 [16384, 4], P(('area', 'dev')), may hold values from 0 to 31, all different within a row; in each aligned block of 128 rows (0 to 127, 128 to 255, ...) at most 32 rows name the same one
- partner_slot: int32 [16384, 4], P(('area', 'dev')), may hold values from 0 to 127
- cond_index: int32 [16384, 5], P(('area', 'dev')), may hold values from 0 to 7
- remote_block: int32 [16384], P(('area', 'dev')), may hold values from 0 to 127
Outputs:
- voltage: float32 [10, 2097152], P(None, ('area', 'dev'))
- gating: float32 [2, 2097152], P(None, ('area', 'dev'))
Inputs may be any that keep to these rules, and one draw needn't show every extreme that they name: `partners`: each row names 4 different devices; among the rows of one device at most 32 name the same device, and that many do on some device. `initial_state`: voltages in the first row, h in the second, n in the third. `conductance`: entries are non-negative.
All inputs are finite; a program needn't handle non-finite values.
Results may differ from a plain program's by a relative error of at most 0.0021.
Values may be sent and summed in bfloat16 or wider, within the bound.
A program may use at most 128 MiB of HBM per device.

v0:
```python
import jax
import jax.numpy as jnp
from jax import lax
from jax.sharding import PartitionSpec as P

K = 10
ITERS = 2
NEWTON = 3


time_step = 0.05
g_sodium = 35.0
g_potassium = 9.0
g_leakage = 0.1
e_sodium = 5.5
e_potassium = -9.0
e_leakage = -6.5


def shifted(block, axis, distance):
    devices = range(lax.axis_size(axis))
    route = [((i - distance) % len(devices), i) for i in devices]
    return lax.ppermute(block, axis, route)


def relax_gate(value, target, tau):
    return target + (value - target) * jnp.exp(-time_step / tau)


def integrate(initial_state, drive_current, inflow, leakage):
    voltage = initial_state[0]
    inactive = initial_state[1]
    active = initial_state[2]
    history = []
    for number in range(K):
        h_target = jax.nn.sigmoid(-(voltage + 5.8) / 0.7)
        h_tau = 0.6 + 3.0 / jnp.cosh((voltage + 5.8) / 1.4)
        inactive = relax_gate(inactive, h_target, h_tau)
        n_target = jax.nn.sigmoid(voltage + 3.0)
        n_tau = 0.5 + 4.0 / jnp.cosh((voltage + 3.0) / 2.0)
        active = relax_gate(active, n_target, n_tau)
        previous = voltage
        fourth = active**4
        for newton in range(NEWTON):
            opening = jax.nn.sigmoid((voltage + 3.5) / 0.8)
            slope_m = opening * (1.0 - opening) / 0.8
            residual = (
                (voltage - previous) / time_step
                + g_sodium * opening**3 * inactive * (voltage - e_sodium)
                + g_potassium * fourth * (voltage - e_potassium)
                + g_leakage * (voltage - e_leakage)
                + leakage * voltage
                - inflow[number]
                - drive_current[number]
            )
            jacobian = (
                1.0 / time_step
                + g_sodium
                * inactive
                * (3.0 * opening**2 * slope_m * (voltage - e_sodium) + opening**3)
                + g_potassium * fourth
                + g_leakage
                + leakage
            )
            jacobian = jnp.maximum(jacobian, 0.5 / time_step)
            voltage = voltage - residual / jacobian
        history.append(voltage)
    return (jnp.stack(history), jnp.stack([inactive, active]))


def group_links(values, labels_in, kinds_count, blocks_here):
    kind_mask = labels_in[:, 1][None, :] == jnp.arange(kinds_count, dtype=jnp.int32)[:, None]
    place_mask = labels_in[:, 0][None, :] == jnp.arange(blocks_here, dtype=jnp.int32)[:, None]
    selector = (kind_mask[:, None, :] & place_mask[None, :, :]).astype(jnp.float32)
    counts = jnp.sum(selector, axis=2)
    selector = selector.astype(jnp.bfloat16).reshape(kinds_count * blocks_here, -1)
    grouped = jnp.dot(selector, values, preferred_element_type=jnp.float32)
    return (grouped, counts)


def local(
    initial_state,
    waveform_guess,
    drive_current,
    conductance,
    partners,
    partner_slot,
    cond_index,
    remote_block,
):
    blocks_here = partners.shape[0]
    parts_count = partners.shape[1]
    kinds_count = conductance.shape[0]
    block_width = conductance.shape[1]
    row_width = K * block_width
    float_conductance = conductance.astype(jnp.float32)
    column_sums = jnp.sum(float_conductance, axis=1)
    meta_area = jnp.stack([remote_block, cond_index[:, parts_count]], axis=-1)
    inner_kinds = cond_index[:, :parts_count]
    my_index = lax.axis_index("dev")
    waveform = waveform_guess
    voltage = None
    gating = None
    for iteration in range(ITERS):
        blocked = waveform.reshape(K, blocks_here, block_width).transpose(1, 0, 2)
        flat_waves = blocked.reshape(blocks_here, row_width)
        all_waves = lax.all_gather(flat_waves, "dev", axis=0, tiled=True)
        all_partners = lax.all_gather(partners, "dev", axis=0, tiled=True)
        all_slots = lax.all_gather(partner_slot, "dev", axis=0, tiled=True)
        all_kinds = lax.all_gather(inner_kinds, "dev", axis=0, tiled=True)
        hit = (all_partners == my_index).astype(jnp.float32)
        kind_hot = (
            all_kinds[:, :, None] == jnp.arange(kinds_count, dtype=jnp.int32)[None, None, :]
        ).astype(jnp.float32) * hit[:, :, None]
        slot_hot = (
            all_slots[:, :, None] == jnp.arange(blocks_here, dtype=jnp.int32)[None, None, :]
        ).astype(jnp.float32)
        selector = jnp.einsum("rpc,rpt->ctr", kind_hot, slot_hot, precision=lax.Precision.HIGHEST)
        counts_near = jnp.sum(selector, axis=2)
        selector = selector.astype(jnp.bfloat16).reshape(kinds_count * blocks_here, -1)
        grouped_near = jnp.dot(selector, all_waves, preferred_element_type=jnp.float32)
        got_area, got_area_meta = shifted((flat_waves, meta_area), "area", 1)
        grouped_far, counts_far = group_links(got_area, got_area_meta, kinds_count, blocks_here)
        grouped = (grouped_near + grouped_far).reshape(kinds_count, blocks_here, K, block_width)
        counts = counts_near + counts_far
        inflow_blocks = jnp.einsum(
            "cbkn,cnm->kbm", grouped, float_conductance, precision=lax.Precision.HIGHEST
        )
        leakage = jnp.einsum(
            "cb,cm->bm", counts, column_sums, precision=lax.Precision.HIGHEST
        ).reshape(-1)
        inflow, leakage = (inflow_blocks.reshape(K, blocks_here * block_width), leakage)
        voltage, gating = integrate(initial_state, drive_current, inflow, leakage)
        waveform = voltage.astype(jnp.bfloat16)
    return (voltage, gating)


def solution(mesh):
    in_specs = (
        P(None, ("area", "dev")),
        P(None, ("area", "dev")),
        P(None, ("area", "dev")),
        P(),
        P(("area", "dev"), None),
        P(("area", "dev"), None),
        P(("area", "dev"), None),
        P(("area", "dev")),
    )
    out_specs = (P(None, ("area", "dev")), P(None, ("area", "dev")))
    return jax.shard_map(local, mesh=mesh, in_specs=in_specs, out_specs=out_specs, check_vma=False)
```

profile of v0, /device:TPU:1, one launch (start us, length us, event | category | flops | bytes accessed | tf_op | source)
XLA Modules:
  0.0 354.7 jit_solution(1093648815819493043)
XLA Ops:
  14.9 26.5 %all_gather.20 = s32[4096,4]{0,1:T(4,128)S(1)} all-gather(s32[128,4]{0,1:T(4,128)} %param.12), channel_id=1, replica_groups=mesh['area'=4,'dev'=32] {'dev'}, dimensions={0}, use_global_device_ids=true | all-gather | bytes 67584 | tf_op jit(solution)/shard_map/all_gather | solution.py:108
  42.1 23.5 %all_gather.19 = s32[4096,4]{0,1:T(4,128)S(1)} all-gather(s32[128,4]{0,1:T(4,128)S(1)} %slice.97), channel_id=1, replica_groups=mesh['area'=4,'dev'=32] {'dev'}, dimensions={0}, use_global_device_ids=true | all-gather | bytes 67584 | tf_op jit(solution)/shard_map/all_gather | solution.py:110
  67.6 21.9 %all_gather.18 = s32[4096,4]{0,1:T(4,128)S(1)} all-gather(s32[128,4]{0,1:T(4,128)S(1)} %copy-done.2), channel_id=1, replica_groups=mesh['area'=4,'dev'=32] {'dev'}, dimensions={0}, use_global_device_ids=true | all-gather | bytes 67584 | tf_op jit(solution)/shard_map/all_gather | solution.py:109
  91.5 38.8 %bitcast_reduce_fusion = (f32[8,128]{1,0:T(8,128)S(1)}, bf16[4096,128,8]{1,2,0:T(8,128)(2,1)}) fusion(f32[4096,4]{1,0:T(8,128)S(1)} %copy.33, s32[4096,4]{1,0:T(8,128)} %copy.32, s32[4096,4]{1,0:T(8,128)} %copy.31), kind=kOutput, calls=%fused_computation.1 | convolution fusion | flops 212073472 | bytes 8589312 | tf_op jit(solution)/shard_map/rpc,rpt->ctr/dot_general | solution.py:118
  131.0 15.6 %fusion.2 = f32[1024,1280]{1,0:T(8,128)S(1)} fusion(bf16[4096,1280]{0,1:T(8,128)(2,1)} %all-gather.3.cloned.1.call-done, bf16[512,8,8,128]{3,2,1,0:T(8,128)(2,1)} %bitcast.156), kind=kOutput, calls=%fused_computation.4 | convolution fusion | flops 10737418240 | bytes 24117248 | tf_op jit(solution)/shard_map/dot_general | solution.py:121
  146.6 3.2 convolution_add_fusion.1
  149.8 6.0 %copy.35 = f32[1024,1280]{0,1:T(8,128)} copy(f32[1024,1280]{1,0:T(8,128)} %convolution_add_fusion.1) | data formatting | bytes 10485760 | tf_op jit(solution)/shard_map/add | solution.py:124
  155.8 3.8 %copy.44 = f32[160,8,8,128]{3,2,1,0:T(8,128)S(1)} copy(f32[160,8,8,128]{3,1,2,0:T(8,128)} %bitcast.122) | data formatting | bytes 10485760
  159.5 4.4 %convolution_bitcast_fusion.1 = f32[10,128,128]{2,1,0:T(8,128)S(1)} fusion(f32[8,128,10,128]{1,0,3,2:T(8,128)S(1)} %bitcast.124, bf16[8,128,128]{2,1,0:T(8,128)(2,1)S(1)} %copy-done), kind=kOutput, calls=%fused_computation.19 | convolution fusion | flops 2013265920 | bytes 6160384 | tf_op jit(solution)/shard_map/cbkn,cnm->kbm/dot_general | solution.py:126
  164.0 4.7 %multiply_add_fusion.33 = (f32[1,16384]{1,0:T(1,128)S(1)}, f32[1,16384]{1,0:T(1,128)S(1)}, f32[1,16384]{1,0:T(1,128)S(1)}, f32[1,16384]{1,0:T(1,128)S(1)}, f32[1,16384]{1,0:T(1,128)S(1)}, /*index=5*/f32[1,16384]{1,0:T(1,128)S(1)}) fusion(f32[1,16384]{1,0:T(1,128)S(1)} %bitcast.104, f32[1,16384]{1,0:T(1,128)S(1)} %bitcast.153, f32[10,16384]{1,0:T(8,128)} %param.10, ...), kind=kLoop, calls=%fused_computation.613 | loop fusion | flops 2703360 | bytes 786432 | tf_op jit(solution)/shard_map/add | solution.py:27
  168.9 4.2 %multiply_add_fusion.31 = (f32[1,16384]{1,0:T(1,128)S(1)}, f32[1,16384]{1,0:T(1,128)S(1)}, f32[1,16384]{1,0:T(1,128)S(1)}) fusion(f32[1,16384]{1,0:T(1,128)S(1)} %get-tuple-element.53, f32[1,16384]{1,0:T(1,128)S(1)} %bitcast.105, f32[1,16384]{1,0:T(1,128)S(1)} %bitcast.152, f32[1,16384]{1,0:T(1,128)S(1)} %get-tuple-element.54, f32[10,16384]{1,0:T(8,128)} %param.10, ...), kind=kLoop, calls=%fused_computation.603 | loop fusion | flops 2473984 | bytes 589824 | tf_op jit(solution)/shard_map/add | solution.py:27
  173.3 4.2 %multiply_add_fusion.29 = (f32[1,16384]{1,0:T(1,128)S(1)}, f32[1,16384]{1,0:T(1,128)S(1)}, f32[1,16384]{1,0:T(1,128)S(1)}) fusion(f32[1,16384]{1,0:T(1,128)S(1)} %get-tuple-element.50, f32[1,16384]{1,0:T(1,128)S(1)} %bitcast.106, f32[1,16384]{1,0:T(1,128)S(1)} %bitcast.149, f32[1,16384]{1,0:T(1,128)S(1)} %get-tuple-element.51, f32[10,16384]{1,0:T(8,128)} %param.10, ...), kind=kLoop, calls=%fused_computation.593 | loop fusion | flops 2473984 | bytes 589824 | tf_op jit(solution)/shard_map/add | solution.py:27
  177.6 4.6 %multiply_add_fusion.27 = (f32[1,16384]{1,0:T(1,128)S(1)}, f32[1,16384]{1,0:T(1,128)S(1)}, f32[1,16384]{1,0:T(1,128)S(1)}) fusion(f32[1,16384]{1,0:T(1,128)S(1)} %get-tuple-element.47, f32[1,16384]{1,0:T(1,128)S(1)} %bitcast.107, f32[1,16384]{1,0:T(1,128)S(1)} %bitcast.147, f32[1,16384]{1,0:T(1,128)S(1)} %get-tuple-element.48, f32[10,16384]{1,0:T(8,128)} %param.10, ...), kind=kLoop, calls=%fused_computation.583 | loop fusion | flops 2473984 | bytes 589824 | tf_op jit(solution)/shard_map/add | solution.py:27
  182.4 4.2 %multiply_add_fusion.25 = (f32[1,16384]{1,0:T(1,128)S(1)}, f32[1,16384]{1,0:T(1,128)S(1)}, f32[1,16384]{1,0:T(1,128)S(1)}) fusion(f32[1,16384]{1,0:T(1,128)S(1)} %get-tuple-element.44, f32[1,16384]{1,0:T(1,128)S(1)} %bitcast.108, f32[1,16384]{1,0:T(1,128)S(1)} %bitcast.145, f32[1,16384]{1,0:T(1,128)S(1)} %get-tuple-element.45, f32[10,16384]{1,0:T(8,128)} %param.10, ...), kind=kLoop, calls=%fused_computation.573 | loop fusion | flops 2473984 | bytes 589824 | tf_op jit(solution)/shard_map/add | solution.py:27
  186.8 4.2 %multiply_add_fusion.23 = (f32[1,16384]{1,0:T(1,128)S(1)}, f32[1,16384]{1,0:T(1,128)S(1)}, f32[1,16384]{1,0:T(1,128)S(1)}) fusion(f32[1,16384]{1,0:T(1,128)S(1)} %get-tuple-element.41, f32[1,16384]{1,0:T(1,128)S(1)} %bitcast.109, f32[1,16384]{1,0:T(1,128)S(1)} %bitcast.142, f32[1,16384]{1,0:T(1,128)S(1)} %get-tuple-element.42, f32[10,16384]{1,0:T(8,128)} %param.10, ...), kind=kLoop, calls=%fused_computation.563 | loop fusion | flops 2473984 | bytes 589824 | tf_op jit(solution)/shard_map/add | solution.py:27
  191.2 4.2 %multiply_add_fusion.21 = (f32[1,16384]{1,0:T(1,128)S(1)}, f32[1,16384]{1,0:T(1,128)S(1)}, f32[1,16384]{1,0:T(1,128)S(1)}) fusion(f32[1,16384]{1,0:T(1,128)S(1)} %get-tuple-element.38, f32[1,16384]{1,0:T(1,128)S(1)} %bitcast.110, f32[1,16384]{1,0:T(1,128)S(1)} %bitcast.140, f32[1,16384]{1,0:T(1,128)S(1)} %get-tuple-element.39, f32[10,16384]{1,0:T(8,128)} %param.10, ...), kind=kLoop, calls=%fused_computation.553 | loop fusion | flops 2473984 | bytes 589824 | tf_op jit(solution)/shard_map/add | solution.py:27
  195.6 7.2 %divide_subtract_fusion.32 = (f32[1,16384]{1,0:T(1,128)S(1)}, f32[1,16384]{1,0:T(1,128)S(1)}, f32[1,16384]{1,0:T(1,128)S(1)}, bf16[1,16384]{1,0:T(2,128)(2,1)S(1)}) fusion(f32[1,16384]{1,0:T(1,128)S(1)} %bitcast.111, f32[1,16384]{1,0:T(1,128)S(1)} %bitcast.136, f32[10,16384]{1,0:T(8,128)} %param.10, f32[1,16384]{1,0:T(1,128)S(1)} %get-tuple-element.35, ...), kind=kLoop, calls=%fused_computation.537 | loop fusion | flops 4734976 | bytes 753664 | tf_op jit(solution)/shard_map/sub | solution.py:66
  203.2 4.5 %convert_reduce_fusion.2 = (bf16[16384]{0:T(1024)(128)(2,1)S(1)}, bf16[16384]{0:T(1024)(128)(2,1)S(1)}) fusion(f32[1,16384]{1,0:T(1,128)S(1)} %bitcast.112, f32[1,16384]{1,0:T(1,128)S(1)} %bitcast.135, f32[1,16384]{1,0:T(1,128)S(1)} %get-tuple-element.31, f32[1,16384]{1,0:T(1,128)S(1)} %get-tuple-element.33, f32[1,16384]{1,0:T(1,128)S(1)} %get-tuple-element.32, ...), kind=kLoop, calls=%fused_computation.528 | loop fusion | flops 2506752 | bytes 458752 | tf_op jit(solution)/shard_map/convert.10
  209.7 61.9 %all-gather.5.cloned.1.call-done = bf16[4096,1280]{0,1:T(8,128)(2,1)} async-done(((bf16[128,1280]{0,1:T(8,128)(2,1)}), bf16[4096,1280]{0,1:T(8,128)(2,1)}) %all-gather.5.cloned.1.call-update) | async-done | bytes 10485776 | tf_op jit(solution)/shard_map/all_gather | solution.py:107
  271.5 15.6 %fusion = f32[1024,1280]{1,0:T(8,128)S(1)} fusion(bf16[4096,1280]{0,1:T(8,128)(2,1)} %all-gather.5.cloned.1.call-done, bf16[512,8,8,128]{3,2,1,0:T(8,128)(2,1)} %bitcast.157), kind=kOutput, calls=%fused_computation.2 | convolution fusion | flops 10737418240 | bytes 24117248 | tf_op jit(solution)/shard_map/dot_general | solution.py:121
  287.1 3.2 convolution_add_fusion
  290.3 6.0 %copy.38 = f32[1024,1280]{0,1:T(8,128)} copy(f32[1024,1280]{1,0:T(8,128)} %convolution_add_fusion) | data formatting | bytes 10485760 | tf_op jit(solution)/shard_map/add | solution.py:124
  296.3 3.8 %copy.45 = f32[160,8,8,128]{3,2,1,0:T(8,128)S(1)} copy(f32[160,8,8,128]{3,1,2,0:T(8,128)} %bitcast.123) | data formatting | bytes 10485760
  300.0 4.4 %convolution_bitcast_fusion = f32[10,128,128]{2,1,0:T(8,128)S(1)} fusion(f32[8,128,10,128]{1,0,3,2:T(8,128)S(1)} %bitcast.125, bf16[8,128,128]{2,1,0:T(8,128)(2,1)S(1)} %copy-done), kind=kOutput, calls=%fused_computation.18 | convolution fusion | flops 2013265920 | bytes 6160384 | tf_op jit(solution)/shard_map/cbkn,cnm->kbm/dot_general | solution.py:126
  307.6 4.2 %multiply_add_fusion.14 = (f32[1,16384]{1,0:T(1,128)S(1)}, f32[1,16384]{1,0:T(1,128)S(1)}, f32[1,16384]{1,0:T(1,128)S(1)}) fusion(f32[1,16384]{1,0:T(1,128)S(1)} %get-tuple-element.29, f32[1,16384]{1,0:T(1,128)S(1)} %bitcast.114, f32[1,16384]{1,0:T(1,128)S(1)} %bitcast.151, f32[1,16384]{1,0:T(1,128)S(1)} %get-tuple-element.30, f32[10,16384]{1,0:T(8,128)} %param.10, ...), kind=kLoop, calls=%fused_computation.511 | loop fusion | flops 2473984 | bytes 589824 | tf_op jit(solution)/shard_map/add | solution.py:27
  311.8 4.2 %multiply_add_fusion.12 = (f32[1,16384]{1,0:T(1,128)S(1)}, f32[1,16384]{1,0:T(1,128)S(1)}, f32[1,16384]{1,0:T(1,128)S(1)}) fusion(f32[1,16384]{1,0:T(1,128)S(1)} %get-tuple-element.26, f32[1,16384]{1,0:T(1,128)S(1)} %bitcast.115, f32[1,16384]{1,0:T(1,128)S(1)} %bitcast.150, f32[1,16384]{1,0:T(1,128)S(1)} %get-tuple-element.27, f32[10,16384]{1,0:T(8,128)} %param.10, ...), kind=kLoop, calls=%fused_computation.502 | loop fusion | flops 2473984 | bytes 589824 | tf_op jit(solution)/shard_map/add | solution.py:27
  316.0 4.2 %multiply_add_fusion.10 = (f32[1,16384]{1,0:T(1,128)S(1)}, f32[1,16384]{1,0:T(1,128)S(1)}, f32[1,16384]{1,0:T(1,128)S(1)}) fusion(f32[1,16384]{1,0:T(1,128)S(1)} %get-tuple-element.23, f32[1,16384]{1,0:T(1,128)S(1)} %bitcast.116, f32[1,16384]{1,0:T(1,128)S(1)} %bitcast.148, f32[1,16384]{1,0:T(1,128)S(1)} %get-tuple-element.24, f32[10,16384]{1,0:T(8,128)} %param.10, ...), kind=kLoop, calls=%fused_computation.493 | loop fusion | flops 2473984 | bytes 589824 | tf_op jit(solution)/shard_map/add | solution.py:27
  320.2 4.4 %multiply_add_fusion.8 = (f32[1,16384]{1,0:T(1,128)S(1)}, f32[1,16384]{1,0:T(1,128)S(1)}, f32[1,16384]{1,0:T(1,128)S(1)}) fusion(f32[1,16384]{1,0:T(1,128)S(1)} %get-tuple-element.20, f32[1,16384]{1,0:T(1,128)S(1)} %bitcast.117, f32[1,16384]{1,0:T(1,128)S(1)} %bitcast.146, f32[1,16384]{1,0:T(1,128)S(1)} %get-tuple-element.21, f32[10,16384]{1,0:T(8,128)} %param.10, ...), kind=kLoop, calls=%fused_computation.484 | loop fusion | flops 2473984 | bytes 589824 | tf_op jit(solution)/shard_map/add | solution.py:27
  324.6 4.2 %multiply_add_fusion.6 = (f32[1,16384]{1,0:T(1,128)S(1)}, f32[1,16384]{1,0:T(1,128)S(1)}, f32[1,16384]{1,0:T(1,128)S(1)}) fusion(f32[1,16384]{1,0:T(1,128)S(1)} %get-tuple-element.17, f32[1,16384]{1,0:T(1,128)S(1)} %bitcast.118, f32[1,16384]{1,0:T(1,128)S(1)} %bitcast.144, f32[1,16384]{1,0:T(1,128)S(1)} %get-tuple-element.18, f32[10,16384]{1,0:T(8,128)} %param.10, ...), kind=kLoop, calls=%fused_computation.475 | loop fusion | flops 2473984 | bytes 589824 | tf_op jit(solution)/shard_map/add | solution.py:27
  328.8 4.2 %multiply_add_fusion.4 = (f32[1,16384]{1,0:T(1,128)S(1)}, f32[1,16384]{1,0:T(1,128)S(1)}, f32[1,16384]{1,0:T(1,128)S(1)}) fusion(f32[1,16384]{1,0:T(1,128)S(1)} %get-tuple-element.14, f32[1,16384]{1,0:T(1,128)S(1)} %bitcast.119, f32[1,16384]{1,0:T(1,128)S(1)} %bitcast.143, f32[1,16384]{1,0:T(1,128)S(1)} %get-tuple-element.15, f32[10,16384]{1,0:T(8,128)} %param.10, ...), kind=kLoop, calls=%fused_computation.466 | loop fusion | flops 2473984 | bytes 589824 | tf_op jit(solution)/shard_map/add | solution.py:27
  333.0 4.2 %multiply_add_fusion.2 = (f32[1,16384]{1,0:T(1,128)S(1)}, f32[1,16384]{1,0:T(1,128)S(1)}, f32[1,16384]{1,0:T(1,128)S(1)}) fusion(f32[1,16384]{1,0:T(1,128)S(1)} %get-tuple-element.11, f32[1,16384]{1,0:T(1,128)S(1)} %bitcast.120, f32[1,16384]{1,0:T(1,128)S(1)} %bitcast.141, f32[1,16384]{1,0:T(1,128)S(1)} %get-tuple-element.12, f32[10,16384]{1,0:T(8,128)} %param.10, ...), kind=kLoop, calls=%fused_computation.457 | loop fusion | flops 2473984 | bytes 589824 | tf_op jit(solution)/shard_map/add | solution.py:27
  337.2 7.3 %divide_subtract_fusion = (f32[1,16384]{1,0:T(1,128)S(1)}, f32[1,16384]{1,0:T(1,128)S(1)}, f32[1,16384]{1,0:T(1,128)S(1)}, f32[1,16384]{1,0:T(1,128)S(1)}) fusion(f32[1,16384]{1,0:T(1,128)S(1)} %bitcast.121, f32[1,16384]{1,0:T(1,128)S(1)} %bitcast.139, f32[10,16384]{1,0:T(8,128)} %param.10, f32[1,16384]{1,0:T(1,128)S(1)} %get-tuple-element.8, ...), kind=kLoop, calls=%fused_computation.442 | loop fusion | flops 4718592 | bytes 786432 | tf_op jit(solution)/shard_map/sub | solution.py:66
  (57 shorter events, 22.7 us)
Async XLA Ops:
  7.2 60.4 %copy-start.2 = (s32[128,4]{0,1:T(4,128)S(1)}, s32[128,4]{0,1:T(4,128)}, u32[]{:S(2)}) copy-start(s32[128,4]{0,1:T(4,128)} %param.13) | copy-start | bytes 6148
  7.2 123.8 %all-gather.3.cloned.1.call-start = ((), (), s32[]{:S(2)}) async-start(), calls=%async_computation | async-start | bytes 10813440 | tf_op jit(solution)/shard_map/all_gather | solution.py:107
  9.3 262.2 %all-gather.5.cloned.1.call-start = ((), (), s32[]{:S(2)}) async-start(), calls=%async_computation.1 | async-start | bytes 10813440 | tf_op jit(solution)/shard_map/all_gather | solution.py:107
  9.4 137.2 %collective-permute-start.1 = (bf16[128,1280]{0,1:T(8,128)(2,1)}, bf16[128,1280]{0,1:T(8,128)(2,1)S(1)}, u32[]{:S(2)}, u32[]{:S(2)}) collective-permute-start(bf16[128,1280]{0,1:T(8,128)(2,1)} %bitcast.130), channel_id=1, source_target_pairs={{96,0},{0,32},{32,64},{64,96},{97,1},{1,33},{33,65},{65,97},{98,2}... | collective-permute-start | bytes 983048 | tf_op jit(solution)/shard_map/ppermute | solution.py:23
  12.9 117.4 %collective-permute-start = (s32[128,2]{0,1:T(2,128)S(1)}, s32[128,2]{0,1:T(2,128)S(1)}, u32[]{:S(2)}, u32[]{:S(2)}) collective-permute-start(s32[128,2]{0,1:T(2,128)S(1)} %pad_add_fusion), channel_id=1, source_target_pairs={{96,0},{0,32},{32,64},{64,96},{97,1},{1,33},{33,65},{65,97},{98,2}... | collective-permute-start | bytes 3080 | tf_op jit(solution)/shard_map/ppermute | solution.py:23
  91.5 38.9 %copy-start = (bf16[8,128,128]{2,1,0:T(8,128)(2,1)S(1)}, bf16[8,128,128]{2,1,0:T(8,128)(2,1)}, u32[]{:S(2)}) copy-start(bf16[8,128,128]{2,1,0:T(8,128)(2,1)} %param.11) | copy-start | bytes 786436
  159.5 4.5 %copy-start.1 = (f32[3,16384]{1,0:T(4,128)S(1)}, f32[3,16384]{1,0:T(4,128)}, u32[]{:S(2)}) copy-start(f32[3,16384]{1,0:T(4,128)} %param.8) | copy-start | bytes 589828
  208.6 78.5 %collective-permute-start.2 = (bf16[128,1280]{0,1:T(8,128)(2,1)}, bf16[128,1280]{0,1:T(8,128)(2,1)S(1)}, u32[]{:S(2)}, u32[]{:S(2)}) collective-permute-start(bf16[128,1280]{0,1:T(8,128)(2,1)} %bitcast.132), channel_id=1, source_target_pairs={{96,0},{0,32},{32,64},{64,96},{97,1},{1,33},{33,65},{65,97},{98,2}... | collective-permute-start | bytes 983048 | tf_op jit(solution)/shard_map/ppermute | solution.py:23
Sparse Core Ops, SparseCore 0:
  10.8 68.7 all-gather.2
  208.7 62.7 all-gather.4
where the time goes:
time: 359 us; the launch traced here: 355 us
  matrix products  85.4 us (24%)
  other arithmetic  85 us (24%)
  blocking collectives  72 us (20%)
  waiting for transfers between devices  61.9 us (17%)
  local copies, waits for them, and re-layouts  31.2 us (9%)
  between operations  14.6 us (4%)
  starting transfers between devices  4.63 us (1%)
    add x15, other arithmetic, relax_gate(): return target + (value - target) * jnp.exp(-time_step / tau)  63 us
    all_gather x2, waiting for transfers between devices, local(): all_waves = lax.all_gather(flat_waves, 'dev', axis=0, tiled=True)  61.9 us
    dot_general x1, matrix products, local(): jnp.einsum('rpc,rpt->ctr', kind_hot, slot_hot, precision=lax.Precision.HI...  38.8 us
    dot_general x2, matrix products, local(): jnp.dot(selector, all_waves, preferred_element_type=jnp.float32)  31.2 us
    all_gather x1, blocking collectives, local(): all_partners = lax.all_gather(partners, 'dev', axis=0, tiled=True)  26.5 us
    all_gather x1, blocking collectives, local(): all_kinds = lax.all_gather(inner_kinds, 'dev', axis=0, tiled=True)  23.5 us
    all_gather x1, blocking collectives, local(): all_slots = lax.all_gather(partner_slot, 'dev', axis=0, tiled=True)  21.9 us
    sub x2, other arithmetic, integrate(): voltage = voltage - residual / jacobian  14.5 us
  transfers between devices with their start and end apart: 5, of which 1 were waited for; matrix products, arithmetic and copies ran while one was open for 22% of the time, Pallas kernels for 0%

commit v1 on v0

v1 whole, which is shorter than its diff:
```python
import functools

import jax
import jax.numpy as jnp
from jax import lax
from jax.experimental import pallas as pl
from jax.experimental.pallas import tpu as pltpu
from jax.sharding import PartitionSpec as P

MESH = pl.DeviceIdType.MESH
K = 10
ITERS = 2
NEWTON = 3
CHUNKS = K * ITERS
NB = 128
CAP = 32
KINDS = 8
AHEAD_GATHER = 4
AHEAD_SELECT = 2
LOG2E = 1.4426950408889634
BF = jnp.bfloat16
F32 = jnp.float32
I32 = jnp.int32


def place():
    area = lax.axis_index("area")
    dev = lax.axis_index("dev")
    core = dev % 2
    z = dev // 8
    x = (dev // 2) % 4
    first = z * (1 - core) + x * core
    second = x * (1 - core) + z * core
    first_unit = 8 * (1 - core) + 2 * core
    second_unit = 2 * (1 - core) + 8 * core
    return area, core, first, second, first_unit, second_unit


def device_at(by_area=0, by_first=0, by_second=0, by_core=0):
    area, core, first, second, first_unit, second_unit = place()
    dev = (
        ((first + by_first) % 4) * first_unit
        + ((second + by_second) % 4) * second_unit
        + (core + by_core) % 2
    )
    return ((area + by_area) % 4, dev)


def rcp(value):
    return pl.reciprocal(value, approx=True)


def gate_pair(shifted, scale):
    u = jnp.exp2(jnp.minimum(shifted * (LOG2E * scale), 20.0 * LOG2E))
    return u, 1.0 + u * u


def step_neurons(v, h, n, leak, drive_in):
    u, bottom = gate_pair(v + 5.8, 1.0 / 1.4)
    target = rcp(bottom)
    tau = 0.6 + 6.0 * (u * target)
    h = target + (h - target) * jnp.exp2((-0.05 * LOG2E) * rcp(tau))
    u, bottom = gate_pair(v + 3.0, -0.5)
    target = rcp(bottom)
    tau = 0.5 + 8.0 * (u * target)
    n = target + (n - target) * jnp.exp2((-0.05 * LOG2E) * rcp(tau))
    square = n * n
    potassium = 9.0 * (square * square)
    linear = leak + potassium + 20.1
    offset = 20.0 * v - 9.0 * potassium - 0.65 + drive_in
    sodium = 35.0 * h
    for _ in range(NEWTON):
        m = rcp(1.0 + jnp.exp2(v * (-1.25 * LOG2E) - 3.5 * 1.25 * LOG2E))
        q = sodium * (m * m * m)
        w = v - 5.5
        residual = linear * v - offset + q * w
        jacobian = linear + q * (1.0 + (3.75 * w) * (1.0 - m))
        v = v - residual * rcp(jnp.maximum(jacobian, 10.0))
    return v, h, n


def kernel(
    wave0, drive, state, cond, lists, volt, gate,
    ag, picked, rcv, select, group, now, leak, m1s, m1r, m2s, m2r,
    send1, recv1, send2, recv2, sendy, recvy, sendm1, recvm1, sendm2, recvm2,
):
    area, core, first, second, first_unit, second_unit = place()
    barrier = pltpu.get_barrier_semaphore()
    greet = [device_at(by_first=o, by_core=c) for o in (1, 2, 3) for c in (0, 1)]
    greet += [device_at(by_second=o, by_core=c) for o in (1, 2, 3) for c in (0, 1)]
    greet += [device_at(by_core=1), device_at(by_area=1), device_at(by_area=3)]
    for other in greet:
        pl.semaphore_signal(barrier, inc=1, device_id=other, device_id_type=MESH)

    for k in range(K):
        ag[k, 0] = wave0[k]
    rows = lax.broadcasted_iota(I32, (32, NB), 0)
    target = (
        ((first + (rows >> 3)) & 3) * first_unit
        + ((second + ((rows >> 1) & 3)) & 3) * second_unit
        + ((core + rows) & 1)
    )
    hit = jnp.zeros((32, NB), F32)
    slot = jnp.zeros((32, NB), I32)
    kind = jnp.zeros((32, NB), I32)
    for p in range(4):
        same = lists[p : p + 1, :] == target
        hit = jnp.where(same, 1.0, hit)
        slot = jnp.where(same, lists[4 + p : 5 + p, :], slot)
        kind = jnp.where(same, lists[8 + p : 9 + p, :], kind)
    before = lax.broadcasted_iota(I32, (NB, NB), 0) < lax.broadcasted_iota(I32, (NB, NB), 1)
    rank = jnp.dot(hit.astype(BF), jnp.where(before, 1.0, 0.0).astype(BF), preferred_element_type=F32)
    rank = jnp.where(hit > 0.5, rank, -1.0).astype(I32)
    for o in range(4):
        part = slice(8 * o, 8 * o + 8)
        put = m1r.at[0] if o == 0 else m1s.at[o]
        put[0] = rank[part]
        put[1] = slot[part]
        put[2] = kind[part]
    m2s[0, 0] = jnp.broadcast_to(lists[13:14, :] + 1, (8, NB))
    m2s[0, 1] = jnp.broadcast_to(lists[12:13, :], (8, NB))

    pl.semaphore_wait(barrier, len(greet))

    def remote(src, dst, send, recv, **where):
        return pltpu.make_async_remote_copy(
            src_ref=src, dst_ref=dst, send_sem=send, recv_sem=recv,
            device_id=device_at(**where), device_id_type=MESH,
        )

    def gather(s):
        for o in (1, 3, 2):
            remote(ag.at[s, 0], ag.at[s, o], send1.at[s], recv1.at[s], by_first=o).start()
        remote(ag.at[s, 0], rcv.at[s, pl.ds(8 * NB, NB)], sendy.at[s], recvy.at[s], by_area=1).start()

    def spread(s):
        for j in (2, 3, 6, 7, 4, 5, 1):
            remote(
                picked.at[s, j - 1], rcv.at[s, pl.ds(j * NB, NB)], send2.at[s], recv2.at[s],
                by_second=j // 2, by_core=j % 2,
            ).start()

    def all_gathered(s):
        return remote(ag.at[s, pl.ds(1, 3)], ag.at[s, pl.ds(1, 3)], send1.at[s], recv1.at[s], by_first=1)

    def all_spread(s):
        return remote(picked.at[s], rcv.at[s, pl.ds(NB, 7 * NB)], send2.at[s], recv2.at[s], by_core=1)

    def all_far(s):
        return remote(ag.at[s, 0], rcv.at[s, pl.ds(8 * NB, NB)], sendy.at[s], recvy.at[s], by_area=1)

    for o in (1, 2, 3):
        remote(m1s.at[o], m1r.at[o], sendm1.at[o], recvm1.at[o], by_first=o).start()
    gather(0)
    remote(m2s.at[0], m2r.at[8], sendm2.at[0], recvm2.at[0], by_area=1).start()
    for s in range(1, AHEAD_GATHER):
        gather(s)
    for o in (1, 2, 3):
        remote(m1s.at[o], m1r.at[o], sendm1.at[o], recvm1.at[o], by_first=o).wait()

    spot = lax.broadcasted_iota(I32, (CAP, NB), 0)
    for o in range(4):
        for j in range(8):
            chosen = m1r[o, 0, j : j + 1, :] == spot
            select[o, j * CAP : (j + 1) * CAP, :] = jnp.where(chosen, 1.0, 0.0).astype(BF)

    def pick(s):
        all_gathered(s).wait_recv()
        for o in range(4):
            got = jnp.dot(select[o], ag[s, o], preferred_element_type=F32).astype(BF)
            part = pl.ds(o * CAP, CAP)
            rcv[s, part, :] = got[:CAP]
            for j in range(1, 8):
                picked[s, j - 1, part, :] = got[j * CAP : (j + 1) * CAP]
        spread(s)

    for s in range(AHEAD_SELECT):
        pick(s)
        gather(AHEAD_GATHER + s)

    meta = jnp.zeros((16, NB), F32)
    diagonal = (lax.broadcasted_iota(I32, (16, 256), 0) & 7) == (lax.broadcasted_iota(I32, (16, 256), 1) >> 5)
    for o in range(4):
        valid = m1r[o, 0] >= 0
        codes = jnp.concatenate(
            [jnp.where(valid, m1r[o, 1] + 1, 0), jnp.where(valid, m1r[o, 2], 0)], axis=0
        ).astype(F32).astype(BF)
        crossed = lax.dot_general(
            codes, select[o], (((1,), (1,)), ((), ())), preferred_element_type=F32
        )
        crossed = jnp.where(diagonal, crossed, 0.0).astype(BF)
        fold = (lax.broadcasted_iota(I32, (256, NB), 0) & 31) + 32 * o == lax.broadcasted_iota(I32, (256, NB), 1)
        meta = meta + jnp.dot(crossed, jnp.where(fold, 1.0, 0.0).astype(BF), preferred_element_type=F32)
    meta = meta.astype(I32)
    for j in range(8):
        put = m2r.at[0] if j == 0 else m2s.at[j]
        put[0] = jnp.broadcast_to(meta[j : j + 1, :], (8, NB))
        put[1] = jnp.broadcast_to(meta[8 + j : 9 + j, :], (8, NB))

    def send_meta(j):
        return remote(
            m2s.at[j], m2r.at[j], sendm2.at[j], recvm2.at[j], by_second=j // 2, by_core=j % 2
        )

    for j in range(1, 8):
        send_meta(j).start()
    for j in range(1, 8):
        send_meta(j).wait()
    remote(m2s.at[0], m2r.at[8], sendm2.at[0], recvm2.at[0], by_area=1).wait()

    cell = lax.broadcasted_iota(I32, (KINDS * NB, NB), 0)
    for j in range(9):
        place1 = m2r[j, 0, 0:1, :]
        code = jnp.where(place1 > 0, m2r[j, 1, 0:1, :] * NB + place1 - 1, -1)
        group[:, j * NB : (j + 1) * NB] = jnp.where(cell == code, 1.0, 0.0).astype(BF)
    counts = jnp.dot(group[...], jnp.ones((9 * NB, NB), BF), preferred_element_type=F32)
    total = jnp.zeros((NB, NB), F32)
    for c in range(KINDS):
        column = jnp.sum(cond[c].astype(F32), axis=0, keepdims=True)
        total = total + counts[c * NB : (c + 1) * NB] * column
    leak[...] = total

    def chunk(s, carry):
        k = s % K

        @pl.when(s + AHEAD_SELECT < CHUNKS)
        def _():
            pick(s + AHEAD_SELECT)

        @pl.when(s + AHEAD_SELECT + AHEAD_GATHER < CHUNKS)
        def _():
            gather(s + AHEAD_SELECT + AHEAD_GATHER)

        @pl.when(k == 0)
        def _():
            now[...] = state[...]

        all_spread(s).wait_recv()
        all_far(s).wait_recv()
        grouped = jnp.dot(group[...], rcv[s], preferred_element_type=F32)
        high = grouped.astype(BF)
        low = (grouped - high.astype(F32)).astype(BF)
        high = jnp.concatenate([high[c * NB : (c + 1) * NB] for c in range(KINDS)], axis=1)
        low = jnp.concatenate([low[c * NB : (c + 1) * NB] for c in range(KINDS)], axis=1)
        table = cond[...].reshape(KINDS * NB, NB)
        inflow = jnp.dot(high, table, preferred_element_type=F32) + jnp.dot(
            low, table, preferred_element_type=F32
        )
        part_rows = 64
        for g in range(NB // part_rows):
            part = slice(g * part_rows, (g + 1) * part_rows)
            v, h, n = step_neurons(
                now[0, part], now[1, part], now[2, part], leak[part], inflow[part] + drive[k, part]
            )
            now[0, part] = v
            now[1, part] = h
            now[2, part] = n
            volt[k, part] = v

        @pl.when(s < K)
        def _():
            ag[s + K, 0] = now[0].astype(BF)

        return carry

    lax.fori_loop(0, CHUNKS, chunk, 0)
    gate[...] = now[1:3]

    def drain(s, carry):
        all_gathered(s).wait_send()
        all_spread(s).wait_send()
        all_far(s).wait_send()
        return carry

    lax.fori_loop(0, CHUNKS, drain, 0)


def local(
    initial_state, waveform_guess, drive_current, conductance, partners, partner_slot, cond_index, remote_block
):
    wave0 = waveform_guess.reshape(K, NB, NB)
    drive = drive_current.reshape(K, NB, NB)
    state = initial_state.reshape(3, NB, NB)
    lists = jnp.concatenate(
        [partners.T, partner_slot.T, cond_index.T, remote_block[None, :], jnp.zeros((2, NB), I32)], axis=0
    )
    dma = pltpu.SemaphoreType.DMA
    volt, gate = pl.pallas_call(
        kernel,
        out_shape=(jax.ShapeDtypeStruct((K, NB, NB), F32), jax.ShapeDtypeStruct((2, NB, NB), F32)),
        in_specs=[pl.BlockSpec(memory_space=pltpu.VMEM)] * 5,
        out_specs=(pl.BlockSpec(memory_space=pltpu.VMEM),) * 2,
        scratch_shapes=[
            pltpu.VMEM((CHUNKS, 4, NB, NB), BF),
            pltpu.VMEM((CHUNKS, 7, NB, NB), BF),
            pltpu.VMEM((CHUNKS, 9 * NB, NB), BF),
            pltpu.VMEM((4, 8 * CAP, NB), BF),
            pltpu.VMEM((KINDS * NB, 9 * NB), BF),
            pltpu.VMEM((3, NB, NB), F32),
            pltpu.VMEM((NB, NB), F32),
            pltpu.VMEM((4, 3, 8, NB), I32),
            pltpu.VMEM((4, 3, 8, NB), I32),
            pltpu.VMEM((8, 2, 8, NB), I32),
            pltpu.VMEM((9, 2, 8, NB), I32),
            dma((CHUNKS,)), dma((CHUNKS,)), dma((CHUNKS,)), dma((CHUNKS,)), dma((CHUNKS,)), dma((CHUNKS,)),
            dma((4,)), dma((4,)), dma((8,)), dma((8,)),
        ],
        compiler_params=pltpu.CompilerParams(
            collective_id=0, has_side_effects=True, vmem_limit_bytes=48 * 1024 * 1024
        ),
        name="relax",
    )(wave0, drive, state, conductance, lists)
    return volt.reshape(K, NB * NB), gate.reshape(2, NB * NB)


def solution(mesh):
    in_specs = (
        P(None, ("area", "dev")),
        P(None, ("area", "dev")),
        P(None, ("area", "dev")),
        P(),
        P(("area", "dev"), None),
        P(("area", "dev"), None),
        P(("area", "dev"), None),
        P(("area", "dev")),
    )
    out_specs = (P(None, ("area", "dev")), P(None, ("area", "dev")))
    return jax.shard_map(local, mesh=mesh, in_specs=in_specs, out_specs=out_specs, check_vma=False)
```

time: 359 us -> 72.2 us (0.20); the launches traced: 355 us -> 72 us
  matrix products: 85.4 us -> 0 us
  other arithmetic: 85 us -> 0 us
  blocking collectives: 72 us -> 0 us
  Pallas kernels: 0 us -> 64.6 us
  waiting for transfers between devices: 61.9 us -> 0 us
  local copies, waits for them, and re-layouts: 31.2 us -> 6.62 us
  between operations: 14.6 us -> 0.74 us
  starting transfers between devices: 4.63 us -> 0 us
    dot_general x8 -> x0, matrix products: 85.4 us -> none  [the longest x1 38.8 us: local(): jnp.einsum('rpc,rpt->ctr', kind_hot, slot_hot, precision=lax.Precision.HI...]
    all_gather x3 -> x0, blocking collectives: 72 us -> none  [the longest x1 26.5 us: local(): all_partners = lax.all_gather(partners, 'dev', axis=0, tiled=True)]
    pallas_call x0 -> x1, Pallas kernels: none -> 64.6 us  [local(): pl.pallas_call(kernel, out_shape=(jax.ShapeDtypeStruct((K, NB, NB), F32),...]
    add x15 -> x0, other arithmetic: 63 us -> none  [relax_gate(): return target + (value - target) * jnp.exp(-time_step / tau)]
    all_gather x2 -> x0, waiting for transfers between devices: 61.9 us -> none  [local(): all_waves = lax.all_gather(flat_waves, 'dev', axis=0, tiled=True)]
    sub x2 -> x0, other arithmetic: 14.5 us -> none  [integrate(): voltage = voltage - residual / jacobian]
    add x2 -> x0, local copies, waits for them, and re-layouts: 12 us -> none  [local(): grouped_near + grouped_far]
    another operation x10 -> x0, other arithmetic: 7.21 us -> none
  transfers between devices with their start and end apart: 5 -> 0, of which waited for: 1 -> 0; matrix products, arithmetic and copies ran while one was open for 22% -> 0% of each run, Pallas kernels for 0% -> 0%
where the time goes in v1:
time: 72.2 us; the launch traced here: 72 us
  Pallas kernels  64.6 us (89%)
  local copies, waits for them, and re-layouts  6.62 us (9%)
  between operations  0.74 us (1%)
    pallas_call x1, Pallas kernels, local(): pl.pallas_call(kernel, out_shape=(jax.ShapeDtypeStruct((K, NB, NB), F32),...  64.6 us
    unnamed x20, local copies, waits for them, and re-layouts  6.5 us

profile of v1, /device:TPU:1, one launch (start us, length us, event | category | flops | bytes accessed | tf_op | source)
XLA Modules:
  0.0 72.0 jit_solution(17387768547026882958)
XLA Ops:
  0.6 1.4 %copy.11 = f32[2,8,128,128]{3,2,1,0:T(8,128)S(1)} copy(f32[2,8,128,128]{3,1,2,0:T(8,128)} %bitcast.26) | data formatting | bytes 2097152
  2.1 0.0 copy-start.1
  2.1 1.0 %copy-done.1 = bf16[10,16384]{1,0:T(8,128)(2,1)S(1)} copy-done((bf16[10,16384]{1,0:T(8,128)(2,1)S(1)}, bf16[10,16384]{1,0:T(8,128)(2,1)}, u32[]{:S(2)}) %copy-start.1) | copy-done | bytes 327704
  3.1 0.1 copy.10
  3.2 0.0 copy-start.2
  3.2 0.0 copy-start
  3.3 0.9 %copy-done.2 = f32[3,16384]{1,0:T(4,128)S(1)} copy-done((f32[3,16384]{1,0:T(4,128)S(1)}, f32[3,16384]{1,0:T(4,128)}, u32[]{:S(2)}) %copy-start.2) | copy-done | bytes 196632
  4.2 0.0 copy-start.5
  4.2 0.0 copy-start.3
  4.2 0.0 copy-start.4
  4.2 0.0 copy-start.6
  4.2 0.6 copy-done.5
  4.8 0.0 copy-done.3
  4.9 0.0 copy-done.4
  4.9 0.0 copy-done.6
  4.9 0.0 copy-done
  4.9 64.6 %relax.1 = (f32[10,128,128]{2,1,0:T(8,128)S(1)}, f32[2,128,128]{2,1,0:T(8,128)S(1)}) custom-call(bf16[10,128,128]{2,1,0:T(8,128)(2,1)S(1)} %slice.wave0, f32[10,128,128]{2,1,0:T(8,128)S(1)} %slice.1.drive, f32[3,128,128]{2,1,0:T(8,128)S(1)} %bitcast.21, bf16[8,128,128]{2,1,0:T(8,128)(2,1)S(1)} %copy-done, s32[16,128]{1,0:T(8,128)S(1)} %concatenate.3.lists), custom_call_target="tpu_custom_call" | custom-call | tf_op jit(solution)/shard_map/relax/pallas_call | solution.py:288
  69.5 0.1 pad
  69.6 1.6 %copy.13 = f32[2,8,128,128]{3,1,2,0:T(8,128)} copy(f32[2,8,128,128]{3,2,1,0:T(8,128)S(1)} %bitcast.23) | data formatting | bytes 2097152
  71.2 0.8 %copy.18 = f32[1,2,128,128]{3,1,2,0:T(2,128)} copy(f32[1,2,128,128]{3,2,1,0:T(8,128)S(1)} %bitcast.22) | data formatting | bytes 262144
  (5 shorter events, 0.1 us)
Async XLA Ops:
  2.1 1.0 %copy-start.1 = (bf16[10,16384]{1,0:T(8,128)(2,1)S(1)}, bf16[10,16384]{1,0:T(8,128)(2,1)}, u32[]{:S(2)}) copy-start(bf16[10,16384]{1,0:T(8,128)(2,1)} %param.9) | copy-start | bytes 983044
  3.2 1.0 %copy-start.2 = (f32[3,16384]{1,0:T(4,128)S(1)}, f32[3,16384]{1,0:T(4,128)}, u32[]{:S(2)}) copy-start(f32[3,16384]{1,0:T(4,128)} %param.8) | copy-start | bytes 589828
  3.2 1.7 %copy-start = (bf16[8,128,128]{2,1,0:T(8,128)(2,1)S(1)}, bf16[8,128,128]{2,1,0:T(8,128)(2,1)}, u32[]{:S(2)}) copy-start(bf16[8,128,128]{2,1,0:T(8,128)(2,1)} %cond.1) | copy-start | bytes 786436
  4.2 0.7 copy-start.5
  4.2 0.7 copy-start.3
  4.2 0.7 copy-start.4
  4.2 0.7 copy-start.6

commit v2 on v1

v2 whole, which is shorter than its diff:
```python
import functools

import jax
import jax.numpy as jnp
from jax import lax
from jax.experimental import pallas as pl
from jax.experimental.pallas import tpu as pltpu
from jax.sharding import PartitionSpec as P

MESH = pl.DeviceIdType.MESH
K = 10
ITERS = 2
NEWTON = 3
CHUNKS = K * ITERS
NB = 128
CAP = 32
KINDS = 8
AHEAD_GATHER = 8
AHEAD_RELAY = 5
AHEAD_SUM = 3
STEPS = 2380.0
MIDDLE = 2.0 * STEPS
EDGE = 10.0 * STEPS
COARSE = 32.0
LOG2E = 1.4426950408889634
BF = jnp.bfloat16
F32 = jnp.float32
I32 = jnp.int32


def rcp(value):
    return pl.reciprocal(value, approx=True)


def gate_pair(shifted, scale):
    u = jnp.exp2(jnp.minimum(shifted * (LOG2E * scale), 20.0 * LOG2E))
    return u, 1.0 + u * u


def step_neurons(v, h, n, leak, drive_in):
    u, bottom = gate_pair(v + 5.8, 1.0 / 1.4)
    target = rcp(bottom)
    tau = 0.6 + 6.0 * (u * target)
    h = target + (h - target) * jnp.exp2((-0.05 * LOG2E) * rcp(tau))
    u, bottom = gate_pair(v + 3.0, -0.5)
    target = rcp(bottom)
    tau = 0.5 + 8.0 * (u * target)
    n = target + (n - target) * jnp.exp2((-0.05 * LOG2E) * rcp(tau))
    square = n * n
    potassium = 9.0 * (square * square)
    linear = leak + potassium + 20.1
    offset = 20.0 * v - 9.0 * potassium - 0.65 + drive_in
    sodium = 35.0 * h
    for _ in range(NEWTON):
        m = rcp(1.0 + jnp.exp2(v * (-1.25 * LOG2E) - 3.5 * 1.25 * LOG2E))
        q = sodium * (m * m * m)
        w = v - 5.5
        residual = linear * v - offset + q * w
        jacobian = linear + q * (1.0 + (3.75 * w) * (1.0 - m))
        v = v - residual * rcp(jnp.maximum(jacobian, 10.0))
    return v, h, n


def dot(a, b, precision=None):
    return jnp.dot(a, b, preferred_element_type=F32, precision=precision)


def dot_last(a, b):
    return lax.dot_general(a, b, (((1,), (1,)), ((), ())), preferred_element_type=F32)


def kernel(
    wave0, drive, state, cond, lists, volt, gate,
    ag, far, sums_out, sums_in, own, select, masks, odd, place, tables, now, leak, enc, dec, left, m1s, m1r, mys, myr, m2s, m2r,
    send1, recv1, sendr, recvr, recvy, send2, recv2, sendm1, recvm1, sendmy, recvmy, sendm2, recvm2,
):
    dev = lax.axis_index("dev")
    core, x, z = dev % 2, (dev // 2) % 4, dev // 8
    area = lax.axis_index("area")
    over_z = [((z + o) % 4) * 8 + x * 2 for o in range(4)]
    column = [(area, over_z[o] + (core + c) % 2) for c in (0, 1) for o in range(4)]
    along = [(area, z * 8 + ((x + o) % 4) * 2 + core) for o in range(4)]
    sibling = column[4]
    next_area = ((area + 1) % 4, dev)
    barrier = pltpu.get_barrier_semaphore()
    greet = column[1:] + along[1:] + [next_area, ((area + 3) % 4, dev)]
    for other in greet:
        pl.semaphore_signal(barrier, inc=1, device_id=other, device_id_type=MESH)

    for k in range(K):
        ag[k, 0] = wave0[k]
    rows = lax.broadcasted_iota(I32, (32, NB), 0)
    target = ((z + (rows >> 3)) & 3) * 8 + ((x + rows) & 3) * 2 + ((core + (rows >> 2)) & 1)
    hit = jnp.zeros((32, NB), F32)
    slot = jnp.zeros((32, NB), I32)
    kind = jnp.zeros((32, NB), I32)
    for p in range(4):
        same = lists[p : p + 1, :] == target
        hit = jnp.where(same, 1.0, hit)
        slot = jnp.where(same, lists[4 + p : 5 + p, :], slot)
        kind = jnp.where(same, lists[8 + p : 9 + p, :], kind)
    lane = lax.broadcasted_iota(I32, (NB, NB), 1)
    line = lax.broadcasted_iota(I32, (NB, NB), 0)
    rank = dot(hit.astype(BF), jnp.where(line < lane, 1.0, 0.0).astype(BF))
    rank = jnp.where(hit > 0.5, rank, -1.0).astype(I32)
    for o in range(4):
        part = slice(8 * o, 8 * o + 8)
        put = m1r.at[0] if o == 0 else m1s.at[o]
        put[0] = rank[part]
        put[1] = slot[part]
        put[2] = kind[part]
    m1s[0] = m1r[0]
    mys[...] = lists[8:16, :]

    pl.semaphore_wait(barrier, len(greet))

    def remote(src, dst, send, recv, where):
        return pltpu.make_async_remote_copy(
            src_ref=src, dst_ref=dst, send_sem=send, recv_sem=recv,
            device_id=where, device_id_type=MESH,
        )

    def gather(s):
        mine = ag.at[s, 0]
        for o in (1, 3, 2):
            remote(mine, ag.at[s, o], send1.at[s], recv1.at[s], column[o]).start()
        remote(mine, ag.at[s, 4], send1.at[s], recvr.at[s], sibling).start()
        remote(mine, far.at[s], send1.at[s], recvy.at[s], next_area).start()

    def relay_copy(s):
        return remote(ag.at[s, pl.ds(1, 3)], ag.at[s, pl.ds(5, 3)], sendr.at[s], recvr.at[s], sibling)

    def relay(s):
        all_gathered(s).wait_recv()
        relay_copy(s).start()

    def spread(s):
        for o in (1, 3, 2):
            remote(sums_out.at[s, o - 1], sums_in.at[s, o - 1], send2.at[s], recv2.at[s], along[o]).start()

    def all_gathered(s):
        return remote(ag.at[s, pl.ds(1, 3)], ag.at[s, pl.ds(1, 3)], send1.at[s], recv1.at[s], column[1])

    def all_sent(s):
        return remote(ag.at[s, pl.ds(0, 5)], ag.at[s, pl.ds(0, 5)], send1.at[s], recv1.at[s], column[1])

    def all_relayed(s):
        return remote(ag.at[s, pl.ds(4, 4)], ag.at[s, pl.ds(4, 4)], sendr.at[s], recvr.at[s], sibling)

    def far_copy(s):
        return remote(ag.at[s, 0], far.at[s], send1.at[s], recvy.at[s], next_area)

    def all_spread(s):
        return remote(sums_out.at[s], sums_in.at[s], send2.at[s], recv2.at[s], along[1])

    def list_copy(b):
        return remote(m1s.at[b % 4], m1r.at[b], sendm1.at[b], recvm1.at[b], column[b])

    far_lists = remote(mys, myr, sendmy, recvmy, next_area)
    for b in range(1, 8):
        list_copy(b).start()
    far_lists.start()
    for s in range(AHEAD_GATHER):
        gather(s)
    for b in range(1, 8):
        list_copy(b).wait()
    far_lists.wait()

    spot = lax.broadcasted_iota(I32, (CAP, NB), 0)
    ones = jnp.ones((NB, NB), BF)
    blocks = [[] for _ in range(4)]
    kinds = [[] for _ in range(4)]
    for b in range(8):
        for d in range(4):
            row = (b // 4) * 4 + d
            chosen = m1r[b, 0, row : row + 1, :] == spot
            select[b, d * CAP : (d + 1) * CAP, :] = jnp.where(chosen, 1.0, 0.0).astype(BF)
            blocks[d].append(jnp.where(chosen, m1r[b, 1, row : row + 1, :] + 1, 0).astype(F32))
            kinds[d].append(jnp.where(chosen, m1r[b, 2, row : row + 1, :], 0).astype(F32))
    for s in range(AHEAD_RELAY):
        relay(s)
    links = []
    for d in range(4):
        for half in (0, 1):
            pieces = slice(4 * half, 4 * half + 4)
            links.append((
                jnp.concatenate(blocks[d][pieces], axis=0).astype(BF), jnp.concatenate(kinds[d][pieces], axis=0).astype(BF)
            ))
    links.append((
        jnp.where(line == lane, myr[5:6, :] + 1, 0).astype(F32).astype(BF),
        jnp.where(line == lane, myr[4:5, :], 0).astype(F32).astype(BF),
    ))
    for c in range(KINDS):
        tables[(c // 2) * NB : (c // 2 + 1) * NB, (c % 2) * NB : (c % 2 + 1) * NB] = cond[c]
    column_sums = [jnp.sum(cond[c].astype(F32), axis=0, keepdims=True) for c in range(KINDS)]
    column_sums = jnp.concatenate(column_sums + [jnp.zeros((NB - KINDS, NB), F32)], axis=0)
    eye = jnp.where(line == lane, 1.0, 0.0).astype(BF)
    counts = []
    for i, (block, table) in enumerate(links):
        part = slice(i * NB, (i + 1) * NB)
        block = dot(block, ones).astype(I32)
        table = dot(table, ones).astype(I32)
        for g in range(4):
            masks[g, part, :] = jnp.where((table >> 1) == g, 1.0, 0.0).astype(BF)
        odd[part, :] = table & 1
        to_block = dot_last(eye, jnp.where(block == lane + 1, 1.0, 0.0).astype(BF)).astype(BF)
        place[:, part] = to_block
        of_kind = jnp.where((table == lane) & (block > 0), 1.0, 0.0).astype(BF)
        counts.append(dot(to_block, of_kind))
    exact = lax.Precision.HIGHEST
    for d in (1, 2, 3):
        count = counts[2 * d] + counts[2 * d + 1]
        m2s[d - 1] = jnp.transpose(count)[0:8, :]
        remote(m2s.at[d - 1], m2r.at[d - 1], sendm2.at[d - 1], recvm2.at[d - 1], along[d]).start()
        bound = dot(count, column_sums, exact)
        enc[d - 1] = jnp.where(bound > 1e-30, STEPS / bound, 0.0)
    left[...] = jnp.zeros((3, NB, NB), F32)
    leak[...] = dot(counts[0] + counts[1] + counts[8], column_sums, exact)

    def add_up(s):
        all_relayed(s).wait_recv()
        far_copy(s).wait_recv()
        picked = [dot(select[b], ag[s, b]).astype(BF) for b in range(8)]
        waves = [got[d * CAP : (d + 1) * CAP] for d in range(4) for got in picked]
        waves = jnp.concatenate(waves + [far[s]], axis=0)
        both = dot(jnp.concatenate([waves * masks[g] for g in range(4)], axis=1), tables[...])
        message = jnp.where(odd[...] > 0, both[:, NB:], both[:, :NB])
        high = message.astype(BF)
        message = jnp.concatenate([high, (message - high.astype(F32)).astype(BF)], axis=1)
        for d in (1, 3, 2, 0):
            part = slice(2 * d * NB, 2 * (d + 1) * NB)
            total = dot(place[:, part], message[part])
            if d == 0:
                total = total + dot(place[:, 8 * NB :], message[8 * NB :])
            total = total[:, :NB] + total[:, NB:]
            if d == 0:
                own[s] = total
            else:
                code = total * enc[d - 1] + (left[d - 1] + MIDDLE)
                inner = jnp.clip(code, -EDGE, EDGE)
                code = jnp.clip(inner + (code - inner) * (1.0 / COARSE), -32767.0, 32767.0)
                sent = jnp.round(code)
                left[d - 1] = code - sent
                sums_out[s, d - 1] = sent.astype(I32).astype(jnp.int16)
        spread(s)

    for s in range(AHEAD_SUM):
        add_up(s)

    for d in (1, 2, 3):
        remote(m2s.at[d - 1], m2r.at[d - 1], sendm2.at[d - 1], recvm2.at[d - 1], along[d]).wait()
        count = jnp.transpose(jnp.concatenate([m2r[d - 1], jnp.zeros((NB - 8, NB), F32)], axis=0))
        bound = dot(count, column_sums, exact)
        dec[d - 1] = bound * (1.0 / STEPS)
        leak[...] += bound

    def chunk(s, carry):
        k = s % K

        @pl.when(s + AHEAD_GATHER < CHUNKS)
        def _():
            gather(s + AHEAD_GATHER)

        @pl.when(s + AHEAD_RELAY < CHUNKS)
        def _():
            relay(s + AHEAD_RELAY)

        @pl.when(s + AHEAD_SUM < CHUNKS)
        def _():
            add_up(s + AHEAD_SUM)

        @pl.when(k == 0)
        def _():
            now[...] = state[...]

        all_spread(s).wait_recv()
        part_rows = 64
        for g in range(NB // part_rows):
            part = slice(g * part_rows, (g + 1) * part_rows)
            inflow = own[s, part] + drive[k, part]
            for d in range(3):
                code = sums_in[s, d, part].astype(I32).astype(F32)
                code = code + (COARSE - 1.0) * (code - jnp.clip(code, -EDGE, EDGE))
                inflow = inflow + (code - MIDDLE) * dec[d, part]
            v, h, n = step_neurons(now[0, part], now[1, part], now[2, part], leak[part], inflow)
            now[0, part] = v
            now[1, part] = h
            now[2, part] = n
            volt[k, part] = v

        @pl.when(s < K)
        def _():
            ag[s + K, 0] = now[0].astype(BF)

        return carry

    lax.fori_loop(0, CHUNKS, chunk, 0)
    gate[...] = now[1:3]

    def drain(s, carry):
        all_sent(s).wait_send()
        relay_copy(s).wait_send()
        all_spread(s).wait_send()
        return carry

    lax.fori_loop(0, CHUNKS, drain, 0)


def local(
    initial_state, waveform_guess, drive_current, conductance, partners, partner_slot, cond_index, remote_block
):
    wave0 = waveform_guess.reshape(K, NB, NB)
    drive = drive_current.reshape(K, NB, NB)
    state = initial_state.reshape(3, NB, NB)
    lists = jnp.concatenate(
        [partners.T, partner_slot.T, cond_index.T, remote_block[None, :], jnp.zeros((2, NB), I32)], axis=0
    )
    dma = pltpu.SemaphoreType.DMA
    volt, gate = pl.pallas_call(
        kernel,
        out_shape=(jax.ShapeDtypeStruct((K, NB, NB), F32), jax.ShapeDtypeStruct((2, NB, NB), F32)),
        in_specs=[pl.BlockSpec(memory_space=pltpu.VMEM)] * 5,
        out_specs=(pl.BlockSpec(memory_space=pltpu.VMEM),) * 2,
        scratch_shapes=[
            pltpu.VMEM((CHUNKS, 8, NB, NB), BF),
            pltpu.VMEM((CHUNKS, NB, NB), BF),
            pltpu.VMEM((CHUNKS, 3, NB, NB), jnp.int16),
            pltpu.VMEM((CHUNKS, 3, NB, NB), jnp.int16),
            pltpu.VMEM((CHUNKS, NB, NB), F32),
            pltpu.VMEM((8, 4 * CAP, NB), BF),
            pltpu.VMEM((4, 9 * NB, NB), BF),
            pltpu.VMEM((9 * NB, NB), I32),
            pltpu.VMEM((NB, 9 * NB), BF),
            pltpu.VMEM((4 * NB, 2 * NB), BF),
            pltpu.VMEM((3, NB, NB), F32),
            pltpu.VMEM((NB, NB), F32),
            pltpu.VMEM((3, NB, NB), F32),
            pltpu.VMEM((3, NB, NB), F32),
            pltpu.VMEM((3, NB, NB), F32),
            pltpu.VMEM((4, 3, 8, NB), I32),
            pltpu.VMEM((8, 3, 8, NB), I32),
            pltpu.VMEM((8, NB), I32),
            pltpu.VMEM((8, NB), I32),
            pltpu.VMEM((3, 8, NB), F32),
            pltpu.VMEM((3, 8, NB), F32),
            dma((CHUNKS,)), dma((CHUNKS,)), dma((CHUNKS,)), dma((CHUNKS,)), dma((CHUNKS,)), dma((CHUNKS,)), dma((CHUNKS,)),
            dma((8,)), dma((8,)), dma, dma, dma((3,)), dma((3,)),
        ],
        compiler_params=pltpu.CompilerParams(
            collective_id=0, has_side_effects=True, vmem_limit_bytes=48 * 1024 * 1024
        ),
        name="relax",
    )(wave0, drive, state, conductance, lists)
    return volt.reshape(K, NB * NB), gate.reshape(2, NB * NB)


def solution(mesh):
    in_specs = (
        P(None, ("area", "dev")),
        P(None, ("area", "dev")),
        P(None, ("area", "dev")),
        P(),
        P(("area", "dev"), None),
        P(("area", "dev"), None),
        P(("area", "dev"), None),
        P(("area", "dev")),
    )
    out_specs = (P(None, ("area", "dev")), P(None, ("area", "dev")))
    return jax.shard_map(local, mesh=mesh, in_specs=in_specs, out_specs=out_specs, check_vma=False)
```

time: 72.2 us -> 62.1 us (0.86); the launches traced: 72 us -> 60.9 us
  Pallas kernels: 64.6 us -> 53.6 us
    pallas_call x1, Pallas kernels: 64.6 us -> 53.6 us  [local(): pl.pallas_call(kernel, out_shape=(jax.ShapeDtypeStruct((K, NB, NB), F32),...]
where the time goes in v2:
time: 62.1 us; the launch traced here: 60.9 us
  Pallas kernels  53.6 us (86%)
  local copies, waits for them, and re-layouts  6.62 us (11%)
  between operations  0.74 us (1%)
    pallas_call x1, Pallas kernels, local(): pl.pallas_call(kernel, out_shape=(jax.ShapeDtypeStruct((K, NB, NB), F32),...  53.6 us
    unnamed x20, local copies, waits for them, and re-layouts  6.5 us

profile of v2, /device:TPU:1, one launch (start us, length us, event | category | flops | bytes accessed | tf_op | source)
XLA Modules:
  0.0 60.9 jit_solution(5354248667833238830)
XLA Ops:
  0.6 1.4 %copy.11 = f32[2,8,128,128]{3,2,1,0:T(8,128)S(1)} copy(f32[2,8,128,128]{3,1,2,0:T(8,128)} %bitcast.26) | data formatting | bytes 2097152
  2.1 0.0 copy-start.1
  2.1 1.0 %copy-done.1 = bf16[10,16384]{1,0:T(8,128)(2,1)S(1)} copy-done((bf16[10,16384]{1,0:T(8,128)(2,1)S(1)}, bf16[10,16384]{1,0:T(8,128)(2,1)}, u32[]{:S(2)}) %copy-start.1) | copy-done | bytes 327704
  3.1 0.1 copy.10
  3.2 0.0 copy-start.2
  3.2 0.0 copy-start
  3.3 0.9 %copy-done.2 = f32[3,16384]{1,0:T(4,128)S(1)} copy-done((f32[3,16384]{1,0:T(4,128)S(1)}, f32[3,16384]{1,0:T(4,128)}, u32[]{:S(2)}) %copy-start.2) | copy-done | bytes 196632
  4.2 0.0 copy-start.5
  4.2 0.0 copy-start.3
  4.2 0.0 copy-start.4
  4.2 0.0 copy-start.6
  4.2 0.6 %copy-done.5 = s32[128,4]{0,1:T(4,128)S(1)} copy-done((s32[128,4]{0,1:T(4,128)S(1)}, s32[128,4]{0,1:T(4,128)}, u32[]{:S(2)}) %copy-start.5) | copy-done | bytes 2072
  4.8 0.0 copy-done.3
  4.9 0.0 copy-done.4
  4.9 0.0 copy-done.6
  4.9 0.0 copy-done
  4.9 53.6 %relax.1 = (f32[10,128,128]{2,1,0:T(8,128)S(1)}, f32[2,128,128]{2,1,0:T(8,128)S(1)}) custom-call(bf16[10,128,128]{2,1,0:T(8,128)(2,1)S(1)} %slice.wave0, f32[10,128,128]{2,1,0:T(8,128)S(1)} %slice.1.drive, f32[3,128,128]{2,1,0:T(8,128)S(1)} %bitcast.21, bf16[8,128,128]{2,1,0:T(8,128)(2,1)S(1)} %copy-done, s32[16,128]{1,0:T(8,128)S(1)} %concatenate.3.lists), custom_call_target="tpu_custom_call" | custom-call | tf_op jit(solution)/shard_map/relax/pallas_call | solution.py:319
  58.5 0.1 pad
  58.6 1.6 %copy.13 = f32[2,8,128,128]{3,1,2,0:T(8,128)} copy(f32[2,8,128,128]{3,2,1,0:T(8,128)S(1)} %bitcast.23) | data formatting | bytes 2097152
  60.1 0.8 %copy.18 = f32[1,2,128,128]{3,1,2,0:T(2,128)} copy(f32[1,2,128,128]{3,2,1,0:T(8,128)S(1)} %bitcast.22) | data formatting | bytes 262144
  (5 shorter events, 0.1 us)
Async XLA Ops:
  2.1 1.0 %copy-start.1 = (bf16[10,16384]{1,0:T(8,128)(2,1)S(1)}, bf16[10,16384]{1,0:T(8,128)(2,1)}, u32[]{:S(2)}) copy-start(bf16[10,16384]{1,0:T(8,128)(2,1)} %param.9) | copy-start | bytes 983044
  3.2 1.0 %copy-start.2 = (f32[3,16384]{1,0:T(4,128)S(1)}, f32[3,16384]{1,0:T(4,128)}, u32[]{:S(2)}) copy-start(f32[3,16384]{1,0:T(4,128)} %param.8) | copy-start | bytes 589828
  3.2 1.7 %copy-start = (bf16[8,128,128]{2,1,0:T(8,128)(2,1)S(1)}, bf16[8,128,128]{2,1,0:T(8,128)(2,1)}, u32[]{:S(2)}) copy-start(bf16[8,128,128]{2,1,0:T(8,128)(2,1)} %cond.1) | copy-start | bytes 786436
  4.2 0.7 %copy-start.5 = (s32[128,4]{0,1:T(4,128)S(1)}, s32[128,4]{0,1:T(4,128)}, u32[]{:S(2)}) copy-start(s32[128,4]{0,1:T(4,128)} %param.13) | copy-start | bytes 6148
  4.2 0.7 %copy-start.3 = (s32[128,5]{0,1:T(8,128)S(1)}, s32[128,5]{0,1:T(8,128)}, u32[]{:S(2)}) copy-start(s32[128,5]{0,1:T(8,128)} %param.14) | copy-start | bytes 7684
  4.2 0.7 %copy-start.4 = (s32[128,4]{0,1:T(4,128)S(1)}, s32[128,4]{0,1:T(4,128)}, u32[]{:S(2)}) copy-start(s32[128,4]{0,1:T(4,128)} %param.12) | copy-start | bytes 6148
  4.2 0.7 %copy-start.6 = (s32[128]{0:T(128)S(1)}, s32[128]{0:T(128)}, u32[]{:S(2)}) copy-start(s32[128]{0:T(128)} %param.15) | copy-start | bytes 1540

commit v3 on v2

--- a/solution.py
+++ b/solution.py
@@ -15,9 +15,9 @@
 NB = 128
 CAP = 32
 KINDS = 8
-AHEAD_GATHER = 8
-AHEAD_RELAY = 5
-AHEAD_SUM = 3
+AHEAD_GATHER = 9
+AHEAD_RELAY = 6
+AHEAD_SUM = 4
 STEPS = 2380.0
 MIDDLE = 2.0 * STEPS
 EDGE = 10.0 * STEPS
@@ -61,8 +61,8 @@
     return v, h, n
 
 
-def dot(a, b, precision=None):
-    return jnp.dot(a, b, preferred_element_type=F32, precision=precision)
+def dot(a, b):
+    return jnp.dot(a, b, preferred_element_type=F32)
 
 
 def dot_last(a, b):
@@ -70,9 +70,9 @@
 
 
 def kernel(
-    wave0, drive, state, cond, lists, volt, gate,
-    ag, far, sums_out, sums_in, own, select, masks, odd, place, tables, now, leak, enc, dec, left, m1s, m1r, mys, myr, m2s, m2r,
-    send1, recv1, sendr, recvr, recvy, send2, recv2, sendm1, recvm1, sendmy, recvmy, sendm2, recvm2,
+    wave_in, drive_in, state_in, cond_in, partners_in, slots_in, kinds_in, remote_in, volt_out, gate_out,
+    wave0, volt_raw, gate_raw, volt, partners, slots, kinds, remotes, drive_raw, state_raw, cond, waves_f32, drive, state, ag, far, sums_out, sums_in, own, select, masks, odd, place, tables, now, leak, enc, dec, left, m1s, m1r, mys, myr, m2s, m2r,
+    load, store, send1, recv1, sendr, recvr, recvy, send2, recv2, sendm1, recvm1, sendmy, recvmy, sendm2, recvm2,
 ):
     dev = lax.axis_index("dev")
     core, x, z = dev % 2, (dev // 2) % 4, dev // 8
@@ -82,23 +82,35 @@
     along = [(area, z * 8 + ((x + o) % 4) * 2 + core) for o in range(4)]
     sibling = column[4]
     next_area = ((area + 1) % 4, dev)
+    loads = [
+        pltpu.make_async_copy(cond_in, cond, load.at[0]),
+        pltpu.make_async_copy(state_in, state_raw, load.at[1]),
+        pltpu.make_async_copy(drive_in, drive_raw, load.at[2]),
+        pltpu.make_async_copy(wave_in, wave0, load.at[3]),
+        pltpu.make_async_copy(partners_in, partners, load.at[4]),
+        pltpu.make_async_copy(slots_in, slots, load.at[5]),
+        pltpu.make_async_copy(kinds_in, kinds, load.at[6]),
+        pltpu.make_async_copy(remote_in, remotes, load.at[7]),
+    ]
+    for item in loads:
+        item.start()
     barrier = pltpu.get_barrier_semaphore()
     greet = column[1:] + along[1:] + [next_area, ((area + 3) % 4, dev)]
     for other in greet:
         pl.semaphore_signal(barrier, inc=1, device_id=other, device_id_type=MESH)
 
-    for k in range(K):
-        ag[k, 0] = wave0[k]
+    for item in loads[4:]:
+        item.wait()
     rows = lax.broadcasted_iota(I32, (32, NB), 0)
     target = ((z + (rows >> 3)) & 3) * 8 + ((x + rows) & 3) * 2 + ((core + (rows >> 2)) & 1)
     hit = jnp.zeros((32, NB), F32)
     slot = jnp.zeros((32, NB), I32)
-    kind = jnp.zeros((32, NB), I32)
+    link_kind = jnp.zeros((32, NB), I32)
     for p in range(4):
-        same = lists[p : p + 1, :] == target
+        same = partners[p : p + 1, :] == target
         hit = jnp.where(same, 1.0, hit)
-        slot = jnp.where(same, lists[4 + p : 5 + p, :], slot)
-        kind = jnp.where(same, lists[8 + p : 9 + p, :], kind)
+        slot = jnp.where(same, slots[p : p + 1, :], slot)
+        link_kind = jnp.where(same, kinds[p : p + 1, :], link_kind)
     lane = lax.broadcasted_iota(I32, (NB, NB), 1)
     line = lax.broadcasted_iota(I32, (NB, NB), 0)
     rank = dot(hit.astype(BF), jnp.where(line < lane, 1.0, 0.0).astype(BF))
@@ -108,9 +120,11 @@
         put = m1r.at[0] if o == 0 else m1s.at[o]
         put[0] = rank[part]
         put[1] = slot[part]
-        put[2] = kind[part]
+        put[2] = link_kind[part]
     m1s[0] = m1r[0]
-    mys[...] = lists[8:16, :]
+    mys[0:1, :] = kinds[4:5, :]
+    mys[1:2, :] = remotes[...]
+    mys[2:8, :] = jnp.zeros((6, NB), I32)
 
     pl.semaphore_wait(barrier, len(greet))
 
@@ -160,8 +174,33 @@
     for b in range(1, 8):
         list_copy(b).start()
     far_lists.start()
-    for s in range(AHEAD_GATHER):
-        gather(s)
+
+    def split_wave(t, carry):
+        column = wave0[:, pl.ds(pl.multiple_of(t * NB, NB), NB)].astype(F32)
+        waves_f32[pl.ds(t, 8, stride=NB), :] = column[0:8]
+        waves_f32[pl.ds(8 * NB + t, 2, stride=NB), :] = column[8:10]
+        return carry
+
+    loads[3].wait()
+    lax.fori_loop(0, NB, split_wave, 0, unroll=8)
+    for s in range(K):
+        ag[s, 0] = waves_f32[s * NB : (s + 1) * NB, :].astype(BF)
+        if s < AHEAD_GATHER:
+            gather(s)
+    loads[0].wait()
+    for c in range(KINDS):
+        tables[(c // 2) * NB : (c // 2 + 1) * NB, (c % 2) * NB : (c % 2 + 1) * NB] = cond[c]
+    column_sums = [jnp.sum(cond[c].astype(F32), axis=0, keepdims=True) for c in range(KINDS)]
+    column_sums = jnp.concatenate(column_sums + [jnp.zeros((NB - KINDS, NB), F32)], axis=0)
+    sums_high = column_sums.astype(BF)
+    column_sums = column_sums - sums_high.astype(F32)
+    sums_mid = column_sums.astype(BF)
+    sums_low = (column_sums - sums_mid.astype(F32)).astype(BF)
+
+    def weigh(count):
+        count = count.astype(BF)
+        return dot(count, sums_high) + (dot(count, sums_mid) + dot(count, sums_low))
+
     for b in range(1, 8):
         list_copy(b).wait()
     far_lists.wait()
@@ -169,31 +208,27 @@
     spot = lax.broadcasted_iota(I32, (CAP, NB), 0)
     ones = jnp.ones((NB, NB), BF)
     blocks = [[] for _ in range(4)]
-    kinds = [[] for _ in range(4)]
+    of_link = [[] for _ in range(4)]
     for b in range(8):
         for d in range(4):
             row = (b // 4) * 4 + d
             chosen = m1r[b, 0, row : row + 1, :] == spot
             select[b, d * CAP : (d + 1) * CAP, :] = jnp.where(chosen, 1.0, 0.0).astype(BF)
             blocks[d].append(jnp.where(chosen, m1r[b, 1, row : row + 1, :] + 1, 0).astype(F32))
-            kinds[d].append(jnp.where(chosen, m1r[b, 2, row : row + 1, :], 0).astype(F32))
-    for s in range(AHEAD_RELAY):
+            of_link[d].append(jnp.where(chosen, m1r[b, 2, row : row + 1, :], 0).astype(F32))
+    for s in range(AHEAD_RELAY - AHEAD_SUM):
         relay(s)
     links = []
     for d in range(4):
         for half in (0, 1):
             pieces = slice(4 * half, 4 * half + 4)
             links.append((
-                jnp.concatenate(blocks[d][pieces], axis=0).astype(BF), jnp.concatenate(kinds[d][pieces], axis=0).astype(BF)
+                jnp.concatenate(blocks[d][pieces], axis=0).astype(BF), jnp.concatenate(of_link[d][pieces], axis=0).astype(BF)
             ))
     links.append((
-        jnp.where(line == lane, myr[5:6, :] + 1, 0).astype(F32).astype(BF),
-        jnp.where(line == lane, myr[4:5, :], 0).astype(F32).astype(BF),
+        jnp.where(line == lane, myr[1:2, :] + 1, 0).astype(F32).astype(BF),
+        jnp.where(line == lane, myr[0:1, :], 0).astype(F32).astype(BF),
     ))
-    for c in range(KINDS):
-        tables[(c // 2) * NB : (c // 2 + 1) * NB, (c % 2) * NB : (c % 2 + 1) * NB] = cond[c]
-    column_sums = [jnp.sum(cond[c].astype(F32), axis=0, keepdims=True) for c in range(KINDS)]
-    column_sums = jnp.concatenate(column_sums + [jnp.zeros((NB - KINDS, NB), F32)], axis=0)
     eye = jnp.where(line == lane, 1.0, 0.0).astype(BF)
     counts = []
     for i, (block, table) in enumerate(links):
@@ -207,15 +242,14 @@
         place[:, part] = to_block
         of_kind = jnp.where((table == lane) & (block > 0), 1.0, 0.0).astype(BF)
         counts.append(dot(to_block, of_kind))
-    exact = lax.Precision.HIGHEST
     for d in (1, 2, 3):
         count = counts[2 * d] + counts[2 * d + 1]
         m2s[d - 1] = jnp.transpose(count)[0:8, :]
         remote(m2s.at[d - 1], m2r.at[d - 1], sendm2.at[d - 1], recvm2.at[d - 1], along[d]).start()
-        bound = dot(count, column_sums, exact)
+        bound = weigh(count)
         enc[d - 1] = jnp.where(bound > 1e-30, STEPS / bound, 0.0)
     left[...] = jnp.zeros((3, NB, NB), F32)
-    leak[...] = dot(counts[0] + counts[1] + counts[8], column_sums, exact)
+    leak[...] = weigh(counts[0] + counts[1]) + weigh(counts[8])
 
     def add_up(s):
         all_relayed(s).wait_recv()
@@ -246,14 +280,43 @@
 
     for s in range(AHEAD_SUM):
         add_up(s)
+        relay(AHEAD_RELAY - AHEAD_SUM + s)
+
+    loads[1].wait()
+    loads[2].wait()
+
+    def split_drive(t, carry):
+        lanes = pl.ds(pl.multiple_of(t * NB, NB), NB)
+        drive[pl.ds(t, 8, stride=NB), :] = drive_raw[0:8, lanes]
+        drive[pl.ds(8 * NB + t, 2, stride=NB), :] = drive_raw[8:10, lanes]
+        state[pl.ds(t, 3, stride=NB), :] = state_raw[:, lanes]
+        return carry
+
+    lax.fori_loop(0, NB, split_drive, 0, unroll=8)
 
     for d in (1, 2, 3):
         remote(m2s.at[d - 1], m2r.at[d - 1], sendm2.at[d - 1], recvm2.at[d - 1], along[d]).wait()
         count = jnp.transpose(jnp.concatenate([m2r[d - 1], jnp.zeros((NB - 8, NB), F32)], axis=0))
-        bound = dot(count, column_sums, exact)
+        bound = weigh(count)
         dec[d - 1] = bound * (1.0 / STEPS)
         leak[...] += bound
 
+    def join_most(t, carry):
+        volt_raw[0:8, pl.ds(pl.multiple_of(t * NB, NB), NB)] = volt[pl.ds(t, 8, stride=NB), :]
+        return carry
+
+    def join_rest(t, carry):
+        lanes = pl.ds(pl.multiple_of(t * NB, NB), NB)
+        volt_raw[8:10, lanes] = volt[pl.ds(8 * NB + t, 2, stride=NB), :]
+        gate_raw[:, lanes] = now[pl.ds(NB + t, 2, stride=NB), :]
+        return carry
+
+    stores = [
+        pltpu.make_async_copy(volt_raw.at[0:8], volt_out.at[0:8], store.at[0]),
+        pltpu.make_async_copy(volt_raw.at[8:10], volt_out.at[8:10], store.at[1]),
+        pltpu.make_async_copy(gate_raw, gate_out, store.at[2]),
+    ]
+
     def chunk(s, carry):
         k = s % K
 
@@ -272,30 +335,39 @@
         @pl.when(k == 0)
         def _():
             now[...] = state[...]
+
+        @pl.when(s == CHUNKS - 2)
+        def _():
+            lax.fori_loop(0, NB, join_most, 0, unroll=8)
+            stores[0].start()
 
         all_spread(s).wait_recv()
         part_rows = 64
         for g in range(NB // part_rows):
-            part = slice(g * part_rows, (g + 1) * part_rows)
-            inflow = own[s, part] + drive[k, part]
+            first = g * part_rows
+            part = slice(first, first + part_rows)
+            inflow = own[s, part] + drive[pl.ds(pl.multiple_of(k * NB + first, part_rows), part_rows), :]
             for d in range(3):
                 code = sums_in[s, d, part].astype(I32).astype(F32)
                 code = code + (COARSE - 1.0) * (code - jnp.clip(code, -EDGE, EDGE))
                 inflow = inflow + (code - MIDDLE) * dec[d, part]
-            v, h, n = step_neurons(now[0, part], now[1, part], now[2, part], leak[part], inflow)
-            now[0, part] = v
-            now[1, part] = h
-            now[2, part] = n
-            volt[k, part] = v
+            v, h, n = (now[i * NB + first : i * NB + first + part_rows] for i in range(3))
+            v, h, n = step_neurons(v, h, n, leak[part], inflow)
+            now[0 * NB + first : 0 * NB + first + part_rows] = v
+            now[1 * NB + first : 1 * NB + first + part_rows] = h
+            now[2 * NB + first : 2 * NB + first + part_rows] = n
+            volt[pl.ds(pl.multiple_of(k * NB + first, part_rows), part_rows), :] = v
 
         @pl.when(s < K)
         def _():
-            ag[s + K, 0] = now[0].astype(BF)
+            ag[s + K, 0] = now[0:NB].astype(BF)
 
         return carry
 
     lax.fori_loop(0, CHUNKS, chunk, 0)
-    gate[...] = now[1:3]
+    lax.fori_loop(0, NB, join_rest, 0, unroll=8)
+    stores[1].start()
+    stores[2].start()
 
     def drain(s, carry):
         all_sent(s).wait_send()
@@ -304,24 +376,34 @@
         return carry
 
     lax.fori_loop(0, CHUNKS, drain, 0)
+    for item in stores:
+        item.wait()
 
 
 def local(
     initial_state, waveform_guess, drive_current, conductance, partners, partner_slot, cond_index, remote_block
 ):
-    wave0 = waveform_guess.reshape(K, NB, NB)
-    drive = drive_current.reshape(K, NB, NB)
-    state = initial_state.reshape(3, NB, NB)
-    lists = jnp.concatenate(
-        [partners.T, partner_slot.T, cond_index.T, remote_block[None, :], jnp.zeros((2, NB), I32)], axis=0
-    )
     dma = pltpu.SemaphoreType.DMA
     volt, gate = pl.pallas_call(
         kernel,
-        out_shape=(jax.ShapeDtypeStruct((K, NB, NB), F32), jax.ShapeDtypeStruct((2, NB, NB), F32)),
-        in_specs=[pl.BlockSpec(memory_space=pltpu.VMEM)] * 5,
-        out_specs=(pl.BlockSpec(memory_space=pltpu.VMEM),) * 2,
+        out_shape=(jax.ShapeDtypeStruct((K, NB * NB), F32), jax.ShapeDtypeStruct((2, NB * NB), F32)),
+        in_specs=[pl.BlockSpec(memory_space=pl.ANY)] * 8,
+        out_specs=(pl.BlockSpec(memory_space=pl.ANY),) * 2,
         scratch_shapes=[
+            pltpu.VMEM((K, NB * NB), BF),
+            pltpu.VMEM((K, NB * NB), F32),
+            pltpu.VMEM((2, NB * NB), F32),
+            pltpu.VMEM((K * NB, NB), F32),
+            pltpu.VMEM((4, NB), I32),
+            pltpu.VMEM((4, NB), I32),
+            pltpu.VMEM((5, NB), I32),
+            pltpu.VMEM((1, NB), I32),
+            pltpu.VMEM((K, NB * NB), F32),
+            pltpu.VMEM((3, NB * NB), F32),
+            pltpu.VMEM((KINDS, NB, NB), BF),
+            pltpu.VMEM((K * NB, NB), F32),
+            pltpu.VMEM((K * NB, NB), F32),
+            pltpu.VMEM((3 * NB, NB), F32),
             pltpu.VMEM((CHUNKS, 8, NB, NB), BF),
             pltpu.VMEM((CHUNKS, NB, NB), BF),
             pltpu.VMEM((CHUNKS, 3, NB, NB), jnp.int16),
@@ -332,7 +414,7 @@
             pltpu.VMEM((9 * NB, NB), I32),
             pltpu.VMEM((NB, 9 * NB), BF),
             pltpu.VMEM((4 * NB, 2 * NB), BF),
-            pltpu.VMEM((3, NB, NB), F32),
+            pltpu.VMEM((3 * NB, NB), F32),
             pltpu.VMEM((NB, NB), F32),
             pltpu.VMEM((3, NB, NB), F32),
             pltpu.VMEM((3, NB, NB), F32),
@@ -343,15 +425,18 @@
             pltpu.VMEM((8, NB), I32),
             pltpu.VMEM((3, 8, NB), F32),
             pltpu.VMEM((3, 8, NB), F32),
-            dma((CHUNKS,)), dma((CHUNKS,)), dma((CHUNKS,)), dma((CHUNKS,)), dma((CHUNKS,)), dma((CHUNKS,)), dma((CHUNKS,)),
+            dma((8,)), dma((3,)), dma((CHUNKS,)), dma((CHUNKS,)), dma((CHUNKS,)), dma((CHUNKS,)), dma((CHUNKS,)), dma((CHUNKS,)), dma((CHUNKS,)),
             dma((8,)), dma((8,)), dma, dma, dma((3,)), dma((3,)),
         ],
         compiler_params=pltpu.CompilerParams(
-            collective_id=0, has_side_effects=True, vmem_limit_bytes=48 * 1024 * 1024
+            collective_id=0, has_side_effects=True, vmem_limit_bytes=60 * 1024 * 1024
         ),
         name="relax",
-    )(wave0, drive, state, conductance, lists)
-    return volt.reshape(K, NB * NB), gate.reshape(2, NB * NB)
+    )(
+        waveform_guess, drive_current, initial_state, conductance,
+        partners.T, partner_slot.T, cond_index.T, remote_block[None, :],
+    )
+    return volt, gate
 
 
 def solution(mesh):

time: 62.1 us -> 55.9 us (0.900); the launches traced: 60.9 us -> 55.7 us
  local copies, waits for them, and re-layouts: 6.62 us -> 2.96 us
  Pallas kernels: 53.6 us -> 52.1 us
    unnamed x20 -> x4, local copies, waits for them, and re-layouts: 6.5 us -> 2.96 us
    pallas_call x1, Pallas kernels: 53.6 us -> 52.1 us  [local(): pl.pallas_call(kernel, out_shape=(jax.ShapeDtypeStruct((K, NB * NB), F32)...]
where the time goes in v3:
time: 55.9 us; the launch traced here: 55.7 us
  Pallas kernels  52.1 us (93%)
  local copies, waits for them, and re-layouts  2.96 us (5%)
  between operations  0.65 us (1%)
    pallas_call x1, Pallas kernels, local(): pl.pallas_call(kernel, out_shape=(jax.ShapeDtypeStruct((K, NB * NB), F32)...  52.1 us
    unnamed x4, local copies, waits for them, and re-layouts  2.96 us

profile of v3, /device:TPU:1, one launch (start us, length us, event | category | flops | bytes accessed | tf_op | source)
XLA Modules:
  0.0 55.7 jit_solution(14864974299611040113)
XLA Ops:
  0.6 52.1 %relax.1 = (f32[10,16384]{1,0:T(8,128)}, f32[2,16384]{1,0:T(2,128)}) custom-call(bf16[10,16384]{1,0:T(8,128)(2,1)} %wave_in.1, f32[10,16384]{1,0:T(8,128)} %drive_in.1, f32[3,16384]{1,0:T(4,128)} %state_in.1, bf16[8,128,128]{2,1,0:T(8,128)(2,1)} %cond_in.1, s32[4,128]{1,0:T(4,128)} %bitcast.5, s32[4,128]{1,0:T(4,128)} %bitcast.6, s32[5,128]{1,0:T(8,128)} %bitcast.4, ...), custom_call_target="tpu_custom_call" | custom-call | tf_op jit(solution)/shard_map/relax/pallas_call | solution.py:387
  52.8 0.0 copy-start
  52.8 2.3 %copy.12 = f32[10,16384]{1,0:T(8,128)} copy(f32[10,16384]{1,0:T(8,128)} %get-tuple-element.4) | data formatting | bytes 1310720
  55.1 0.0 copy-done
  55.1 0.7 %copy.13 = f32[2,16384]{1,0:T(2,128)} copy(f32[2,16384]{1,0:T(2,128)S(1)} %copy-done) | data formatting | bytes 262144
Async XLA Ops:
  52.8 2.3 %copy-start = (f32[2,16384]{1,0:T(2,128)S(1)}, f32[2,16384]{1,0:T(2,128)}, u32[]{:S(2)}) copy-start(f32[2,16384]{1,0:T(2,128)} %get-tuple-element.5) | copy-start | bytes 393220

commit v4 on v3

--- a/solution.py
+++ b/solution.py
@@ -196,10 +196,11 @@
     column_sums = column_sums - sums_high.astype(F32)
     sums_mid = column_sums.astype(BF)
     sums_low = (column_sums - sums_mid.astype(F32)).astype(BF)
+    sums_parts = jnp.concatenate([sums_high, sums_mid, sums_low], axis=1)
 
     def weigh(count):
-        count = count.astype(BF)
-        return dot(count, sums_high) + (dot(count, sums_mid) + dot(count, sums_low))
+        weighed = dot(count.astype(BF), sums_parts)
+        return weighed[:, :NB] + (weighed[:, NB : 2 * NB] + weighed[:, 2 * NB :])
 
     for b in range(1, 8):
         list_copy(b).wait()
@@ -216,40 +217,30 @@
             select[b, d * CAP : (d + 1) * CAP, :] = jnp.where(chosen, 1.0, 0.0).astype(BF)
             blocks[d].append(jnp.where(chosen, m1r[b, 1, row : row + 1, :] + 1, 0).astype(F32))
             of_link[d].append(jnp.where(chosen, m1r[b, 2, row : row + 1, :], 0).astype(F32))
+    eye = jnp.where(line == lane, 1.0, 0.0)
+    blocks = [block for d in range(4) for block in blocks[d]] + [eye * (myr[1:2, :] + 1).astype(F32)]
+    of_link = [table for d in range(4) for table in of_link[d]] + [eye * myr[0:1, :].astype(F32)]
+    block = dot(jnp.concatenate(blocks, axis=0).astype(BF), ones).astype(I32)
+    table = dot(jnp.concatenate(of_link, axis=0).astype(BF), ones).astype(I32)
+    lanes = lax.broadcasted_iota(I32, (9 * NB, NB), 1)
+    place[...] = dot_last(eye.astype(BF), jnp.where(block == lanes + 1, 1.0, 0.0).astype(BF)).astype(BF)
+    for g in range(4):
+        masks[g] = jnp.where((table >> 1) == g, 1.0, 0.0).astype(BF)
+    odd[...] = table & 1
+    of_kind = jnp.where((table == lanes) & (block > 0), 1.0, 0.0).astype(BF)
+    parts = [slice(2 * d * NB, 2 * (d + 1) * NB) for d in range(4)] + [slice(8 * NB, 9 * NB)]
+    counts = [dot(place[:, part], of_kind[part]) for part in parts]
+    bounds = weigh(jnp.concatenate(counts, axis=0))
+    for d in (1, 2, 3):
+        bound = bounds[d * NB : (d + 1) * NB]
+        enc[d - 1] = jnp.where(bound > 1e-30, STEPS / bound, 0.0)
     for s in range(AHEAD_RELAY - AHEAD_SUM):
         relay(s)
-    links = []
-    for d in range(4):
-        for half in (0, 1):
-            pieces = slice(4 * half, 4 * half + 4)
-            links.append((
-                jnp.concatenate(blocks[d][pieces], axis=0).astype(BF), jnp.concatenate(of_link[d][pieces], axis=0).astype(BF)
-            ))
-    links.append((
-        jnp.where(line == lane, myr[1:2, :] + 1, 0).astype(F32).astype(BF),
-        jnp.where(line == lane, myr[0:1, :], 0).astype(F32).astype(BF),
-    ))
-    eye = jnp.where(line == lane, 1.0, 0.0).astype(BF)
-    counts = []
-    for i, (block, table) in enumerate(links):
-        part = slice(i * NB, (i + 1) * NB)
-        block = dot(block, ones).astype(I32)
-        table = dot(table, ones).astype(I32)
-        for g in range(4):
-            masks[g, part, :] = jnp.where((table >> 1) == g, 1.0, 0.0).astype(BF)
-        odd[part, :] = table & 1
-        to_block = dot_last(eye, jnp.where(block == lane + 1, 1.0, 0.0).astype(BF)).astype(BF)
-        place[:, part] = to_block
-        of_kind = jnp.where((table == lane) & (block > 0), 1.0, 0.0).astype(BF)
-        counts.append(dot(to_block, of_kind))
     for d in (1, 2, 3):
-        count = counts[2 * d] + counts[2 * d + 1]
-        m2s[d - 1] = jnp.transpose(count)[0:8, :]
+        m2s[d - 1] = jnp.transpose(counts[d])[0:8, :]
         remote(m2s.at[d - 1], m2r.at[d - 1], sendm2.at[d - 1], recvm2.at[d - 1], along[d]).start()
-        bound = weigh(count)
-        enc[d - 1] = jnp.where(bound > 1e-30, STEPS / bound, 0.0)
     left[...] = jnp.zeros((3, NB, NB), F32)
-    leak[...] = weigh(counts[0] + counts[1]) + weigh(counts[8])
+    leak[...] = bounds[0:NB] + bounds[4 * NB :]
 
     def add_up(s):
         all_relayed(s).wait_recv()
@@ -296,9 +287,12 @@
 
     for d in (1, 2, 3):
         remote(m2s.at[d - 1], m2r.at[d - 1], sendm2.at[d - 1], recvm2.at[d - 1], along[d]).wait()
-        count = jnp.transpose(jnp.concatenate([m2r[d - 1], jnp.zeros((NB - 8, NB), F32)], axis=0))
-        bound = weigh(count)
-        dec[d - 1] = bound * (1.0 / STEPS)
+    rest = jnp.zeros((NB - 8, NB), F32)
+    counts = [jnp.transpose(jnp.concatenate([m2r[d], rest], axis=0)) for d in range(3)]
+    bounds = weigh(jnp.concatenate(counts, axis=0))
+    for d in range(3):
+        bound = bounds[d * NB : (d + 1) * NB]
+        dec[d] = bound * (1.0 / STEPS)
         leak[...] += bound
 
     def join_most(t, carry):
@@ -436,7 +430,32 @@
         waveform_guess, drive_current, initial_state, conductance,
         partners.T, partner_slot.T, cond_index.T, remote_block[None, :],
     )
-    return volt, gate
+
+    def hand_on(volt_in, gate_in, volt_out, gate_out, volt_held, gate_held, taken, done):
+        parts = 4
+        size = NB * NB // parts
+        hops = [(gate_in, gate_held, gate_out)]
+        for i in range(parts):
+            lanes = pl.ds(i * size, size)
+            hops.append((volt_in.at[:, lanes], volt_held.at[:, lanes], volt_out.at[:, lanes]))
+        loads = [pltpu.make_async_copy(a, b, taken.at[i]) for i, (a, b, c) in enumerate(hops)]
+        stores = [pltpu.make_async_copy(b, c, done.at[i]) for i, (a, b, c) in enumerate(hops)]
+        for item in loads:
+            item.start()
+        for i in range(parts + 1):
+            loads[i].wait()
+            stores[i].start()
+        for item in stores:
+            item.wait()
+
+    return pl.pallas_call(
+        hand_on,
+        out_shape=(jax.ShapeDtypeStruct(volt.shape, F32), jax.ShapeDtypeStruct(gate.shape, F32)),
+        in_specs=[pl.BlockSpec(memory_space=pl.ANY)] * 2,
+        out_specs=(pl.BlockSpec(memory_space=pl.ANY),) * 2,
+        scratch_shapes=[pltpu.VMEM(volt.shape, F32), pltpu.VMEM(gate.shape, F32), dma((5,)), dma((5,))],
+        name="hand_on",
+    )(volt, gate)
 
 
 def solution(mesh):

time: 55.9 us -> 52.9 us (0.946)
  local copies, waits for them, and re-layouts: 2.96 us -> 0 us
    unnamed x4 -> x0, local copies, waits for them, and re-layouts: 2.96 us -> none
    pallas_call x1, Pallas kernels: 52.1 us -> 49.6 us  [local(): pl.pallas_call(kernel, out_shape=(jax.ShapeDtypeStruct((K, NB * NB), F32)...]
    pallas_call x0 -> x1, Pallas kernels: none -> 2.07 us  [local(): pl.pallas_call(hand_on, out_shape=(jax.ShapeDtypeStruct(volt.shape, F32),...]
where the time goes in v4:
time: 52.9 us; the launch traced here: 52.3 us
  Pallas kernels  51.7 us (98%)
  between operations  0.64 us (1%)
    pallas_call x1, Pallas kernels, local(): pl.pallas_call(kernel, out_shape=(jax.ShapeDtypeStruct((K, NB * NB), F32)...  49.6 us
    pallas_call x1, Pallas kernels, local(): pl.pallas_call(hand_on, out_shape=(jax.ShapeDtypeStruct(volt.shape, F32),...  2.07 us

profile of v4, /device:TPU:1, one launch (start us, length us, event | category | flops | bytes accessed | tf_op | source)
XLA Modules:
  0.0 52.3 jit_solution(3361484264391854340)
XLA Ops:
  0.6 49.6 %relax.1 = (f32[10,16384]{1,0:T(8,128)}, f32[2,16384]{1,0:T(2,128)}) custom-call(bf16[10,16384]{1,0:T(8,128)(2,1)} %wave_in.1, f32[10,16384]{1,0:T(8,128)} %drive_in.1, f32[3,16384]{1,0:T(4,128)} %state_in.1, bf16[8,128,128]{2,1,0:T(8,128)(2,1)} %cond_in.1, s32[4,128]{1,0:T(4,128)} %bitcast.5, s32[4,128]{1,0:T(4,128)} %bitcast.6, s32[5,128]{1,0:T(8,128)} %bitcast.4, ...), custom_call_target="tpu_custom_call" | custom-call | tf_op jit(solution)/shard_map/relax/pallas_call | solution.py:381
  50.2 2.1 %hand_on.1 = (f32[10,16384]{1,0:T(8,128)}, f32[2,16384]{1,0:T(2,128)}) custom-call(f32[10,16384]{1,0:T(8,128)} %get-tuple-element.4.volt_in, f32[2,16384]{1,0:T(2,128)} %get-tuple-element.5.gate_in), custom_call_target="tpu_custom_call" | custom-call | tf_op jit(solution)/shard_map/hand_on/pallas_call | solution.py:451

commit v5 on v4

--- a/solution.py
+++ b/solution.py
@@ -82,6 +82,11 @@
     along = [(area, z * 8 + ((x + o) % 4) * 2 + core) for o in range(4)]
     sibling = column[4]
     next_area = ((area + 1) % 4, dev)
+    barrier = pltpu.get_barrier_semaphore()
+    greet = column[1:] + along[1:] + [next_area, ((area + 3) % 4, dev)]
+    for other in greet:
+        pl.semaphore_signal(barrier, inc=1, device_id=other, device_id_type=MESH)
+
     loads = [
         pltpu.make_async_copy(cond_in, cond, load.at[0]),
         pltpu.make_async_copy(state_in, state_raw, load.at[1]),
@@ -92,13 +97,8 @@
         pltpu.make_async_copy(kinds_in, kinds, load.at[6]),
         pltpu.make_async_copy(remote_in, remotes, load.at[7]),
     ]
-    for item in loads:
+    for item in loads[4:] + [loads[3], loads[0], loads[1], loads[2]]:
         item.start()
-    barrier = pltpu.get_barrier_semaphore()
-    greet = column[1:] + along[1:] + [next_area, ((area + 3) % 4, dev)]
-    for other in greet:
-        pl.semaphore_signal(barrier, inc=1, device_id=other, device_id_type=MESH)
-
     for item in loads[4:]:
         item.wait()
     rows = lax.broadcasted_iota(I32, (32, NB), 0)
@@ -318,13 +318,13 @@
         def _():
             gather(s + AHEAD_GATHER)
 
+        @pl.when(s + AHEAD_SUM < CHUNKS)
+        def _():
+            add_up(s + AHEAD_SUM)
+
         @pl.when(s + AHEAD_RELAY < CHUNKS)
         def _():
             relay(s + AHEAD_RELAY)
-
-        @pl.when(s + AHEAD_SUM < CHUNKS)
-        def _():
-            add_up(s + AHEAD_SUM)
 
         @pl.when(k == 0)
         def _():

time: 52.9 us -> 52.9 us (level)
  no operation moved by 1% of the time
where the time goes in v5:
time: 52.9 us; the launch traced here: 52.7 us
  Pallas kernels  52.1 us (98%)
  between operations  0.64 us (1%)
    pallas_call x1, Pallas kernels, local(): pl.pallas_call(kernel, out_shape=(jax.ShapeDtypeStruct((K, NB * NB), F32)...  50 us
    pallas_call x1, Pallas kernels, local(): pl.pallas_call(hand_on, out_shape=(jax.ShapeDtypeStruct(volt.shape, F32),...  2.07 us

profile of v5, /device:TPU:1, one launch (start us, length us, event | category | flops | bytes accessed | tf_op | source)
XLA Modules:
  0.0 52.7 jit_solution(2632859194175987135)
XLA Ops:
  0.6 50.0 %relax.1 = (f32[10,16384]{1,0:T(8,128)}, f32[2,16384]{1,0:T(2,128)}) custom-call(bf16[10,16384]{1,0:T(8,128)(2,1)} %wave_in.1, f32[10,16384]{1,0:T(8,128)} %drive_in.1, f32[3,16384]{1,0:T(4,128)} %state_in.1, bf16[8,128,128]{2,1,0:T(8,128)(2,1)} %cond_in.1, s32[4,128]{1,0:T(4,128)} %bitcast.5, s32[4,128]{1,0:T(4,128)} %bitcast.6, s32[5,128]{1,0:T(8,128)} %bitcast.4, ...), custom_call_target="tpu_custom_call" | custom-call | tf_op jit(solution)/shard_map/relax/pallas_call | solution.py:381
  50.6 2.1 %hand_on.1 = (f32[10,16384]{1,0:T(8,128)}, f32[2,16384]{1,0:T(2,128)}) custom-call(f32[10,16384]{1,0:T(8,128)} %get-tuple-element.4.volt_in, f32[2,16384]{1,0:T(2,128)} %get-tuple-element.5.gate_in), custom_call_target="tpu_custom_call" | custom-call | tf_op jit(solution)/shard_map/hand_on/pallas_call | solution.py:451
